TPU v7x, 32 devices: a whole 2x2x4 slice. The times are simulated.
32 devices in a mesh: dp: 16 (over z, y, x), tensor: 2 (over core).
Axes of the slice: x: 2, y: 2, z: 4, core: 2. Of those that a mesh axis runs over, the one named last changes fastest.
Arguments:
- tokens: bfloat16 [32768, 768], P('dp'), may hold values from -6 to 6
- cotangent: bfloat16 [32768, 768], P('dp'), may hold values from -6 to 6
- span_doc: int32 [256], replicated, may hold values from 0 to 191, as said below
- qkv_weight: float32 [768, 3, 768], P('dp', None, 'tensor'), may hold values from -0.21875 to 0.21875
- out_weight: float32 [768, 768], P('tensor', 'dp'), may hold values from -0.625 to 0.625
- ffn_in_weight: float32 [768, 3072], P('dp', 'tensor'), may hold values from -0.21875 to 0.21875
- ffn_out_weight: float32 [3072, 768], P('tensor', 'dp'), may hold values from -0.109375 to 0.109375
- norm_params: float32 [4, 768], P(None, 'dp'), may hold values from -1.2 to 2.5, as said below
- qkv_first: float32 [768, 3, 768], P('dp', None, 'tensor'), may hold values from -0.00061035156 to 0.00061035156
- qkv_second: float32 [768, 3, 768], P('dp', None, 'tensor'), may hold values from 7.061189e-11 to 1.1297903e-09
- out_first: float32 [768, 768], P('tensor', 'dp'), may hold values from -0.00061035156 to 0.00061035156
- out_second: float32 [768, 768], P('tensor', 'dp'), may hold values from 7.061189e-11 to 1.1297903e-09
- ffn_in_first: float32 [768, 3072], P('dp', 'tensor'), may hold values from -0.00061035156 to 0.00061035156
- ffn_in_second: float32 [768, 3072], P('dp', 'tensor'), may hold values from 7.061189e-11 to 1.1297903e-09
- ffn_out_first: float32 [3072, 768], P('tensor', 'dp'), may hold values from -0.00061035156 to 0.00061035156
- ffn_out_second: float32 [3072, 768], P('tensor', 'dp'), may hold values from 7.061189e-11 to 1.1297903e-09
- norm_first: float32 [4, 768], P(None, 'dp'), may hold values from -0.0024414062 to 0.0024414062
- norm_second: float32 [4, 768], P(None, 'dp'), may hold values from 1.1297903e-09 to 1.8076644e-08
Outputs:
- mixed: bfloat16 [32768, 768], P('dp')
- input_grad: float32 [32768, 768], P('dp')
- loss: float32 [], replicated
- clip_norm: float32 [], replicated
- qkv_first_new: float32 [768, 3, 768], P('dp', None, 'tensor')
- qkv_second_new: float32 [768, 3, 768], P('dp', None, 'tensor')
- qkv_weight_new: float32 [768, 3, 768], P('dp', None, 'tensor')
- out_first_new: float32 [768, 768], P('tensor', 'dp')
- out_second_new: float32 [768, 768], P('tensor', 'dp')
- out_weight_new: float32 [768, 768], P('tensor', 'dp')
- ffn_in_first_new: float32 [768, 3072], P('dp', 'tensor')
- ffn_in_second_new: float32 [768, 3072], P('dp', 'tensor')
- ffn_in_weight_new: float32 [768, 3072], P('dp', 'tensor')
- ffn_out_first_new: float32 [3072, 768], P('tensor', 'dp')
- ffn_out_second_new: float32 [3072, 768], P('tensor', 'dp')
- ffn_out_weight_new: float32 [3072, 768], P('tensor', 'dp')
- norm_first_new: float32 [4, 768], P(None, 'dp')
- norm_second_new: float32 [4, 768], P(None, 'dp')
- norm_params_new: float32 [4, 768], P(None, 'dp')
Inputs may be any that keep to these rules, and one draw needn't show every extreme that they name: span_doc never falls along the spans and numbers the documents 0, 1, 2 and so on; each document holds one or two consecutive spans; exactly 64 documents hold two spans, document 0 among them. `norm_params`: rows 0 and 2 are gains, rows 1 and 3 shifts.
All inputs are finite; a program needn't handle non-finite values.
Results may differ from a plain program's by a relative error of at most 0.012.
Values may be sent and summed in bfloat16 or wider, within the bound.
No kernel may reach another device: no remote copies, remote signals or barrier semaphores. Data moves between devices by JAX's collectives and lax.ppermute only.
A program may use at most 192 MiB of HBM per device.

v0:
```python
from functools import partial

import jax
import jax.numpy as jnp
from jax import lax
from jax.sharding import PartitionSpec as P

HEAD = 64
SPAN = 128
STEP = 10


contrast_weight = 4.0


def matmul(left, right):
    return jnp.dot(left, right, precision=lax.Precision.HIGHEST, preferred_element_type=jnp.float32)


def layer_norm(hidden, norm_gain, norm_shift):
    center = hidden - jnp.mean(hidden, axis=-1, keepdims=True)
    spread = jnp.mean(center * center, axis=-1, keepdims=True)
    return center * lax.rsqrt(spread + 1e-06) * norm_gain + norm_shift


def contrast_from_logits(logits, span_doc):
    span_total = logits.shape[0]
    position = jnp.arange(span_total, dtype=jnp.int32)
    itself = position[:, None] == position[None, :]
    partner = jnp.logical_and(span_doc[:, None] == span_doc[None, :], jnp.logical_not(itself))
    masked = jnp.where(itself, -1000000000.0, logits)
    row_max = jnp.max(masked, axis=1, keepdims=True)
    log_total = jnp.log(jnp.sum(jnp.exp(masked - row_max), axis=1)) + row_max[:, 0]
    positive = jnp.sum(jnp.where(partner, logits, 0.0), axis=1)
    flagged = jnp.where(jnp.any(partner, axis=1), 1.0, 0.0)
    return jnp.sum(flagged * (log_total - positive)) / jnp.sum(flagged)


def adam_update(weight, gradient, moment_one, moment_two, step_rate, decay_rate):
    first_new = 0.9 * moment_one + 0.1 * gradient
    second_new = 0.999 * moment_two + 0.001 * gradient * gradient
    corr_first = first_new / (1.0 - 0.9**STEP)
    corr_second = second_new / (1.0 - 0.999**STEP)
    weight_new = weight - step_rate * (
        corr_first / (jnp.sqrt(corr_second) + 1e-08) + decay_rate * weight
    )
    return (first_new, second_new, weight_new)


def tensor_total(partial_rows):
    return lax.psum(partial_rows, "tensor")


def attend_scores(packed):
    return jnp.einsum(
        "nqhe,nkhe->nhqk", packed[:, :, 0], packed[:, :, 1], preferred_element_type=jnp.float32
    ) * HEAD ** (-0.5)


def forward_pass(tokens, weights):
    attn_in, attn_out, ffn_in, ffn_out, norm_rows = weights
    row_count, feature_count = tokens.shape
    span_count = row_count // SPAN
    head_count = attn_in.shape[2] // HEAD
    packed = jnp.dot(
        tokens, attn_in.reshape(feature_count, -1), preferred_element_type=jnp.float32
    ).astype(jnp.bfloat16)
    packed = packed.reshape(span_count, SPAN, 3, head_count, HEAD)
    scores = attend_scores(packed)
    row_max = jnp.max(scores, axis=-1, keepdims=True)
    log_total = row_max + jnp.log(jnp.sum(jnp.exp(scores - row_max), axis=-1, keepdims=True))
    softmaxed = jnp.exp(scores - log_total).astype(jnp.bfloat16)
    context = jnp.einsum(
        "nhqk,nkhe->nqhe", softmaxed, packed[:, :, 2], preferred_element_type=jnp.float32
    )
    context = context.astype(jnp.bfloat16).reshape(row_count, -1)
    attn_part = jnp.dot(context, attn_out, preferred_element_type=jnp.float32)
    norm_gains = norm_rows.astype(jnp.float32)
    attended = tensor_total(attn_part)
    before = tokens.astype(jnp.float32) + attended
    normed = layer_norm(before, norm_gains[0], norm_gains[1])
    normed_low = normed.astype(jnp.bfloat16)
    hidden = jnp.dot(normed_low, ffn_in, preferred_element_type=jnp.float32)
    activated = jax.nn.gelu(hidden, approximate=False).astype(jnp.bfloat16)
    ffn_part = jnp.dot(activated, ffn_out, preferred_element_type=jnp.float32)
    branch_out = tensor_total(ffn_part)
    resid_two = normed + branch_out
    output_low = layer_norm(resid_two, norm_gains[2], norm_gains[3]).astype(jnp.bfloat16)
    return (
        output_low,
        (packed, log_total, context, before, normed_low, hidden, activated, resid_two),
    )


def backward_pass(tokens, weights, saved, grad_output):
    attn_in, attn_out, ffn_in, ffn_out, norm_rows = weights
    packed, log_total, context, before, normed_full, hidden, activated, resid_two = saved
    row_count, feature_count = tokens.shape
    span_count = packed.shape[0]
    head_count = packed.shape[3]
    norm_gains = norm_rows.astype(jnp.float32)
    pull_two = jax.vjp(layer_norm, resid_two, norm_gains[2], norm_gains[3])[1]
    grad_resid, gain_two, shift_two = pull_two(grad_output)
    grad_ffn = grad_resid.astype(jnp.bfloat16)
    grad_down = jnp.dot(activated.T, grad_ffn, preferred_element_type=jnp.float32)
    grad_act = jnp.dot(grad_ffn, ffn_out.T, preferred_element_type=jnp.float32)
    pull_gelu = jax.vjp(partial(jax.nn.gelu, approximate=False), hidden)[1]
    grad_hidden = pull_gelu(grad_act)[0].astype(jnp.bfloat16)
    grad_up = jnp.dot(normed_full.T, grad_hidden, preferred_element_type=jnp.float32)
    back_part = jnp.dot(grad_hidden, ffn_in.T, preferred_element_type=jnp.float32)
    grad_normed = grad_resid + tensor_total(back_part)
    pull_one = jax.vjp(layer_norm, before, norm_gains[0], norm_gains[1])[1]
    grad_before, gain_one, shift_one = pull_one(grad_normed)
    grad_attn = grad_before.astype(jnp.bfloat16)
    grad_proj = jnp.dot(context.T, grad_attn, preferred_element_type=jnp.float32)
    grad_context = jnp.dot(grad_attn, attn_out.T, preferred_element_type=jnp.float32).astype(
        jnp.bfloat16
    )
    grad_context = grad_context.reshape(span_count, SPAN, head_count, HEAD)
    scores = attend_scores(packed)
    soft_full = jnp.exp(scores - log_total)
    softmaxed = soft_full.astype(jnp.bfloat16)
    grad_values = jnp.einsum(
        "nhqk,nqhe->nkhe", softmaxed, grad_context, preferred_element_type=jnp.float32
    )
    grad_soft = jnp.einsum(
        "nqhe,nkhe->nhqk", grad_context, packed[:, :, 2], preferred_element_type=jnp.float32
    )
    grad_scores = soft_full * (grad_soft - jnp.sum(soft_full * grad_soft, axis=-1, keepdims=True))
    grad_scores = grad_scores.astype(jnp.bfloat16)
    grad_queries = jnp.einsum(
        "nhqk,nkhe->nqhe", grad_scores, packed[:, :, 1], preferred_element_type=jnp.float32
    ) * HEAD ** (-0.5)
    grad_keys = jnp.einsum(
        "nhqk,nqhe->nkhe", grad_scores, packed[:, :, 0], preferred_element_type=jnp.float32
    ) * HEAD ** (-0.5)
    grad_packed = (
        jnp.stack([grad_queries, grad_keys, grad_values], axis=2)
        .astype(jnp.bfloat16)
        .reshape(row_count, -1)
    )
    grad_qkv = jnp.dot(tokens.T, grad_packed, preferred_element_type=jnp.float32).reshape(
        attn_in.shape
    )
    input_part = jnp.dot(
        grad_packed, attn_in.reshape(feature_count, -1).T, preferred_element_type=jnp.float32
    )
    norm_all = jnp.stack([gain_one, shift_one, gain_two, shift_two])
    norm_sent = jnp.zeros_like(norm_all)
    input_total, norm_total = (
        lax.psum(input_part.astype(jnp.bfloat16), "tensor").astype(jnp.float32),
        lax.psum(norm_sent.astype(jnp.bfloat16), "tensor").astype(jnp.float32),
    )
    input_grad = grad_before + input_total
    shard_qkv, shard_up = (
        lax.psum_scatter(grad_qkv, "dp", scatter_dimension=0, tiled=True),
        lax.psum_scatter(grad_up, "dp", scatter_dimension=0, tiled=True),
    )
    shard_proj, shard_down, shard_norm = (
        lax.psum_scatter(grad_proj, "dp", scatter_dimension=1, tiled=True),
        lax.psum_scatter(grad_down, "dp", scatter_dimension=1, tiled=True),
        lax.psum_scatter(norm_all, "dp", scatter_dimension=1, tiled=True),
    )
    return (input_grad, (shard_qkv, shard_proj, shard_up, shard_down, shard_norm))


def body(
    tokens,
    cotangent,
    span_doc,
    qkv_weight,
    out_weight,
    ffn_in_weight,
    ffn_out_weight,
    norm_params,
    qkv_first,
    qkv_second,
    out_first,
    out_second,
    ffn_in_first,
    ffn_in_second,
    ffn_out_first,
    ffn_out_second,
    norm_first,
    norm_second,
):
    row_blocks = (
        lax.all_gather(qkv_weight.astype(jnp.bfloat16), "dp", axis=0, tiled=True),
        lax.all_gather(ffn_in_weight.astype(jnp.bfloat16), "dp", axis=0, tiled=True),
    )
    col_blocks = (
        lax.all_gather(out_weight.astype(jnp.bfloat16), "dp", axis=1, tiled=True),
        lax.all_gather(ffn_out_weight.astype(jnp.bfloat16), "dp", axis=1, tiled=True),
        lax.all_gather(norm_params.astype(jnp.bfloat16), "dp", axis=1, tiled=True),
    )
    weights = (row_blocks[0], col_blocks[0], row_blocks[1], col_blocks[1], col_blocks[2])
    row_count = tokens.shape[0]
    span_count = row_count // SPAN
    output_low, saved = forward_pass(tokens, weights)
    cls_local = output_low.reshape(span_count, SPAN, -1)[:, 0, :]
    cls_all = lax.all_gather(cls_local, "dp", axis=0, tiled=True)
    logit_scale = cls_all.shape[1] ** (-0.5)
    logits = jnp.dot(cls_all, cls_all.T, preferred_element_type=jnp.float32) * logit_scale
    contrast_loss, pull_loss = jax.vjp(partial(contrast_from_logits, span_doc=span_doc), logits)
    grad_logits = pull_loss(jnp.asarray(contrast_weight * cls_all.shape[0], dtype=jnp.float32))[0]
    symmetric = grad_logits + grad_logits.T
    own_logits = lax.dynamic_slice_in_dim(
        symmetric, lax.axis_index("dp") * span_count, span_count, 0
    )
    grad_cls = matmul(own_logits, cls_all.astype(jnp.float32)) * logit_scale
    grad_output = cotangent.astype(jnp.float32).reshape(span_count, SPAN, -1)
    grad_output = grad_output.at[:, 0, :].add(grad_cls).reshape(row_count, -1)
    source, grad_output = lax.optimization_barrier((tokens, grad_output))
    saved = forward_pass(source, weights)[1]
    input_grad, shards = backward_pass(source, weights, saved, grad_output)
    tensor_count = lax.axis_size("tensor")
    local_squares = jnp.sum(shards[0] * shards[0]) + jnp.sum(shards[1] * shards[1])
    local_squares = local_squares + jnp.sum(shards[2] * shards[2]) + jnp.sum(shards[3] * shards[3])
    local_squares = local_squares + jnp.sum(shards[4] * shards[4]) / tensor_count
    clip_norm = jnp.sqrt(lax.psum(local_squares, ("dp", "tensor")))
    clip_scale = 1.0 / jnp.maximum(clip_norm, 1.0)
    qkv_new = adam_update(qkv_weight, shards[0] * clip_scale, qkv_first, qkv_second, 0.02, 0.01)
    out_new = adam_update(out_weight, shards[1] * clip_scale, out_first, out_second, 0.02, 0.01)
    up_new = adam_update(
        ffn_in_weight, shards[2] * clip_scale, ffn_in_first, ffn_in_second, 0.02, 0.01
    )
    down_new = adam_update(
        ffn_out_weight, shards[3] * clip_scale, ffn_out_first, ffn_out_second, 0.02, 0.01
    )
    norm_new = adam_update(norm_params, shards[4] * clip_scale, norm_first, norm_second, 0.5, 0.0)
    return (
        output_low,
        input_grad,
        contrast_loss,
        clip_norm,
        qkv_new[0],
        qkv_new[1],
        qkv_new[2],
        out_new[0],
        out_new[1],
        out_new[2],
        up_new[0],
        up_new[1],
        up_new[2],
        down_new[0],
        down_new[1],
        down_new[2],
        norm_new[0],
        norm_new[1],
        norm_new[2],
    )


def solution(mesh):
    placed = (
        P("dp", None),
        P("dp", None),
        P(),
        P("dp", None, "tensor"),
        P("tensor", "dp"),
        P("dp", "tensor"),
        P("tensor", "dp"),
        P(None, "dp"),
        P("dp", None, "tensor"),
        P("dp", None, "tensor"),
        P("tensor", "dp"),
        P("tensor", "dp"),
        P("dp", "tensor"),
        P("dp", "tensor"),
        P("tensor", "dp"),
        P("tensor", "dp"),
        P(None, "dp"),
        P(None, "dp"),
    )
    return jax.shard_map(
        body,
        mesh=mesh,
        in_specs=placed,
        out_specs=(
            P("dp", None),
            P("dp", None),
            P(),
            P(),
            P("dp", None, "tensor"),
            P("dp", None, "tensor"),
            P("dp", None, "tensor"),
            P("tensor", "dp"),
            P("tensor", "dp"),
            P("tensor", "dp"),
            P("dp", "tensor"),
            P("dp", "tensor"),
            P("dp", "tensor"),
            P("tensor", "dp"),
            P("tensor", "dp"),
            P("tensor", "dp"),
            P(None, "dp"),
            P(None, "dp"),
            P(None, "dp"),
        ),
        check_vma=False,
    )
```

profile of v0, /device:TPU:0, one launch (start us, length us, event | category | flops | bytes accessed | tf_op | source)
XLA Modules:
  0.0 1410.5 jit_solution(1463362898277007133)
XLA Ops:
  9.8 46.9 %all_gather.19 = bf16[384,768]{0,1:T(8,128)(2,1)S(1)} all-gather(bf16[384,48]{0,1:T(8,128)(2,1)S(1)} %convert_element_type.112), channel_id=1, replica_groups=mesh['dp'=16,'tensor'=2] {'dp'}, dimensions={1}, use_global_device_ids=true | all-gather | bytes 626688 | tf_op jit(solution)/shard_map/all_gather | solution.py:192
  56.7 16.7 %all-gather.6.cloned.1.call-done = bf16[768,3,384]{2,0,1:T(8,128)(2,1)} async-done(((bf16[48,3,384]{2,0,1:T(8,128)(2,1)}), bf16[768,3,384]{2,0,1:T(8,128)(2,1)}) %all-gather.6.cloned.1.call-update) | async-done | bytes 1769488 | tf_op jit(solution)/shard_map/all_gather | solution.py:188
  110.1 38.5 %all-gather.1 = bf16[16,48,4]{1,2,0:T(4,128)(2,1)S(1)} all-gather(bf16[1,48,4]{1,2,0:T(4,128)(2,1)S(1)} %convert_bitcast_fusion), channel_id=1, replica_groups=mesh['dp'=16,'tensor'=2] {'dp'}, dimensions={0}, use_global_device_ids=true | all-gather | bytes 6528 | tf_op jit(solution)/shard_map/all_gather | solution.py:194
  155.5 50.1 %all-gather.8.cloned.1.call-done = bf16[768,1536]{1,0:T(8,128)(2,1)} async-done(((bf16[48,1536]{1,0:T(8,128)(2,1)}), bf16[768,1536]{1,0:T(8,128)(2,1)}) %all-gather.8.cloned.1.call-update) | async-done | bytes 2359312 | tf_op jit(solution)/shard_map/all_gather | solution.py:189
  205.6 64.7 %all-gather.10.cloned.1.call-done = bf16[1536,768]{0,1:T(8,128)(2,1)} async-done(((bf16[1536,48]{0,1:T(8,128)(2,1)}), bf16[1536,768]{0,1:T(8,128)(2,1)}) %all-gather.10.cloned.1.call-update) | async-done | bytes 2359312 | tf_op jit(solution)/shard_map/all_gather | solution.py:193
  270.3 50.5 %fusion.16 = f32[2048,768]{1,0:T(8,128)} fusion(bf16[1536,768]{0,1:T(8,128)(2,1)} %all-gather.10.cloned.1.call-done, bf16[768,1536]{1,0:T(8,128)(2,1)} %all-gather.8.cloned.1.call-done, f32[768]{0:T(1024)S(1)} %get-tuple-element.45, f32[768]{0:T(1024)S(1)} %get-tuple-element.46, f32[2048]{0:T(1024)S(1)} %add_rsqrt_fusion.1, ...), kind=kOutput, calls=%fused_computation.61 | convolution fusion | flops 9879158784 | bytes 20469760 | tf_op jit(solution)/shard_map/dot_general | solution.py:85
  330.1 21.7 %all-reduce.9.cloned.1.call-done = f32[2048,768]{1,0:T(8,128)} async-done(((f32[2048,768]{1,0:T(8,128)}), f32[2048,768]{1,0:T(8,128)}) %all-reduce.9.cloned.1.call-update) | async-done | bytes 6291472 | tf_op jit(solution)/shard_map/psum | solution.py:51
  361.4 43.2 %all-gather = bf16[256,1,768]{2,0,1:T(8,128)(2,1)S(1)} all-gather(bf16[16,1,768]{2,0,1:T(8,128)(2,1)S(1)} %copy.144), channel_id=2, replica_groups=mesh['dp'=16,'tensor'=2] {'dp'}, dimensions={0}, use_global_device_ids=true | all-gather | bytes 417792 | tf_op jit(solution)/shard_map/all_gather | solution.py:201
  446.8 27.6 %all-reduce.11.cloned.1.call-done = f32[2048,768]{1,0:T(8,128)} async-done(((f32[2048,768]{1,0:T(8,128)}), f32[2048,768]{1,0:T(8,128)}) %all-reduce.11.cloned.1.call-update) | async-done | bytes 6291472 | tf_op jit(solution)/shard_map/psum | solution.py:51
  481.3 33.6 %multiply_convert_fusion = (bf16[2048,1536]{1,0:T(8,128)(2,1)S(1)}, f32[2048,1536]{1,0:T(8,128)}, f32[2048,1536]{1,0:T(8,128)}) fusion(bf16[768,1536]{1,0:T(8,128)(2,1)S(1)} %copy-done.50, f32[2048,768]{1,0:T(8,128)S(1)} %get-tuple-element.74, f32[2048]{0:T(1024)S(1)} %fusion.103, f32[2048]{0:T(1024)S(1)} %broadcast_multiply_fusion.1, ...), kind=kOutput, calls=%fused_computation.7 | convolution fusion | flops 5044174848 | bytes 40130560 | tf_op jit(solution)/shard_map/dot_general | solution.py:83
  524.6 33.3 %all-reduce.13.cloned.1.call-done = f32[2048,768]{1,0:T(8,128)} async-done(((f32[2048,768]{1,0:T(8,128)}), f32[2048,768]{1,0:T(8,128)}) %all-reduce.13.cloned.1.call-update) | async-done | bytes 6291472 | tf_op jit(solution)/shard_map/psum | solution.py:51
  572.1 18.4 %add_convert_fusion = bf16[2048,1536]{1,0:T(8,128)(2,1)} fusion(f32[2048,1536]{1,0:T(8,128)} %get-tuple-element.72, f32[2048,1536]{1,0:T(8,128)} %get-tuple-element.105, bf16[1536,768]{0,1:T(8,128)(2,1)} %all-gather.10.cloned.1.call-done, f32[2048,768]{1,0:T(8,128)S(1)} %get-tuple-element.68, f32[2048]{0:T(1024)S(1)} %negate_multiply_fusion.3), kind=kOutput, calls=%fused_computation.6 | convolution fusion | flops 4879024128 | bytes 40116224 | tf_op jit(solution)/shard_map/dot_general | solution.py:106
  590.4 9.6 fusion.168
  600.2 33.3 %all-reduce.15.cloned.1.call-done = f32[2048,768]{1,0:T(8,128)} async-done(((f32[2048,768]{1,0:T(8,128)}), f32[2048,768]{1,0:T(8,128)}) %all-reduce.15.cloned.1.call-update) | async-done | bytes 6291472 | tf_op jit(solution)/shard_map/psum | solution.py:51
  654.6 10.7 fusion.144
  665.4 12.4 fusion.145
  720.2 9.8 convolution_convert_fusion.2
  731.4 40.0 %reduce-scatter.16.cloned.1.call-done = f32[48,4]{1,0:T(8,128)} async-done(((f32[768,4]{1,0:T(8,128)}), f32[48,4]{1,0:T(8,128)}) %reduce-scatter.16.cloned.1.call-update) | async-done | bytes 784
  773.4 126.0 %reduce-scatter.10.cloned.1.call-done = f32[384,48]{0,1:T(8,128)} async-done(((f32[384,768]{0,1:T(8,128)}), f32[384,48]{0,1:T(8,128)}) %reduce-scatter.10.cloned.1.call-update) | async-done | bytes 73744 | tf_op jit(solution)/shard_map/reduce_scatter | solution.py:160
  900.9 140.8 %reduce-scatter.14.cloned.1.call-done = f32[1536,48]{0,1:T(8,128)} async-done(((f32[1536,768]{0,1:T(8,128)}), f32[1536,48]{0,1:T(8,128)}) %reduce-scatter.14.cloned.1.call-update) | async-done | bytes 294928 | tf_op jit(solution)/shard_map/reduce_scatter | solution.py:161
  1043.4 140.8 %reduce-scatter.12.cloned.1.call-done = f32[48,1536]{1,0:T(8,128)} async-done(((f32[768,1536]{1,0:T(8,128)}), f32[48,1536]{1,0:T(8,128)}) %reduce-scatter.12.cloned.1.call-update) | async-done | bytes 294928 | tf_op jit(solution)/shard_map/reduce_scatter | solution.py:157
  1185.9 137.1 %reduce-scatter.8.cloned.1.call-done = f32[48,3,384]{2,0,1:T(8,128)} async-done(((f32[768,3,384]{2,0,1:T(8,128)}), f32[48,3,384]{2,0,1:T(8,128)}) %reduce-scatter.8.cloned.1.call-update) | async-done | bytes 221200 | tf_op jit(solution)/shard_map/reduce_scatter | solution.py:156
  1327.4 20.3 %all-reduce.17.cloned.1.call-done = bf16[2048,768]{1,0:T(8,128)(2,1)} async-done(((bf16[2048,768]{1,0:T(8,128)(2,1)}), bf16[2048,768]{1,0:T(8,128)(2,1)}) %all-reduce.17.cloned.1.call-update) | async-done | bytes 3145744 | tf_op jit(solution)/shard_map/psum | solution.py:151
  1354.9 40.5 %psum.55 = f32[]{:T(128)} all-reduce(f32[]{:T(128)S(6)} %add.250), channel_id=1, replica_groups=mesh['dp'=16,'tensor'=2] {'dp','tensor'}, use_global_device_ids=true, to_apply=%region_45.46 | all-reduce | flops 1 | bytes 8 | tf_op jit(solution)/shard_map/psum | solution.py:220
  (250 shorter events, 220.2 us)
Async XLA Ops:
  7.2 66.2 %all-gather.6.cloned.1.call-start = ((), (), s32[]{:S(2)}) async-start(), calls=%async_computation.5 | async-start | bytes 1880064 | tf_op jit(solution)/shard_map/all_gather | solution.py:188
  8.9 140.4 %all-reduce.7.cloned.1.call-start = ((), (), s32[]{:S(2)}) async-start(), calls=%async_computation.6 | async-start | bytes 12582912 | tf_op jit(solution)/shard_map/psum | solution.py:51
  107.3 98.2 %all-gather.8.cloned.1.call-start = ((), (), s32[]{:S(2)}) async-start(), calls=%async_computation.7 | async-start | bytes 2506752 | tf_op jit(solution)/shard_map/all_gather | solution.py:189
  108.1 162.2 %all-gather.10.cloned.1.call-start = ((), (), s32[]{:S(2)}) async-start(), calls=%async_computation.8 | async-start | bytes 2506752 | tf_op jit(solution)/shard_map/all_gather | solution.py:193
  110.0 241.8 %all-reduce.9.cloned.1.call-start = ((), (), s32[]{:S(2)}) async-start(), calls=%async_computation.9 | async-start | bytes 12582912 | tf_op jit(solution)/shard_map/psum | solution.py:51
  320.8 153.6 %all-reduce.11.cloned.1.call-start = ((), (), s32[]{:S(2)}) async-start(), calls=%async_computation.10 | async-start | bytes 12582912 | tf_op jit(solution)/shard_map/psum | solution.py:51
  446.3 111.5 %all-reduce.13.cloned.1.call-start = ((), (), s32[]{:S(2)}) async-start(), calls=%async_computation.11 | async-start | bytes 12582912 | tf_op jit(solution)/shard_map/psum | solution.py:51
  524.5 108.9 %all-reduce.15.cloned.1.call-start = ((), (), s32[]{:S(2)}) async-start(), calls=%async_computation.12 | async-start | bytes 12582912 | tf_op jit(solution)/shard_map/psum | solution.py:51
  600.1 171.3 %reduce-scatter.16.cloned.1.call-start = ((), (), s32[]{:S(2)}) async-start(), calls=%async_computation.18 | async-start | bytes 417792
  648.4 251.0 %reduce-scatter.10.cloned.1.call-start = ((), (), s32[]{:S(2)}) async-start(), calls=%async_computation.15 | async-start | bytes 1253376 | tf_op jit(solution)/shard_map/reduce_scatter | solution.py:160
  654.4 387.4 %reduce-scatter.14.cloned.1.call-start = ((), (), s32[]{:S(2)}) async-start(), calls=%async_computation.17 | async-start | bytes 5013504 | tf_op jit(solution)/shard_map/reduce_scatter | solution.py:161
  665.4 518.9 %reduce-scatter.12.cloned.1.call-start = ((), (), s32[]{:S(2)}) async-start(), calls=%async_computation.16 | async-start | bytes 5013504 | tf_op jit(solution)/shard_map/reduce_scatter | solution.py:157
  677.9 645.1 %reduce-scatter.8.cloned.1.call-start = ((), (), s32[]{:S(2)}) async-start(), calls=%async_computation.14 | async-start | bytes 3760128 | tf_op jit(solution)/shard_map/reduce_scatter | solution.py:156
  720.2 627.5 %all-reduce.17.cloned.1.call-start = ((), (), s32[]{:S(2)}) async-start(), calls=%async_computation.13 | async-start | bytes 6291456 | tf_op jit(solution)/shard_map/psum | solution.py:151
  1327.3 70.9 %copy-start.28 = (f32[48,3,384]{2,0,1:T(8,128)S(1)}, f32[48,3,384]{2,0,1:T(8,128)}, u32[]{:S(2)}) copy-start(f32[48,3,384]{2,0,1:T(8,128)} %reduce-scatter.8.cloned.1.call-done) | copy-start | bytes 663556
  1327.3 70.9 %copy-start.29 = (f32[48,3,384]{2,0,1:T(8,128)S(1)}, f32[48,3,384]{2,0,1:T(8,128)}, u32[]{:S(2)}) copy-start(f32[48,3,384]{2,0,1:T(8,128)} %param.23) | copy-start | bytes 663556
  1327.3 71.8 %copy-start.24 = (f32[48,1536]{1,0:T(8,128)S(1)}, f32[48,1536]{1,0:T(8,128)}, u32[]{:S(2)}) copy-start(f32[48,1536]{1,0:T(8,128)} %param.25) | copy-start | bytes 884740
  1327.3 71.8 %copy-start.27 = (f32[48,1536]{1,0:T(8,128)S(1)}, f32[48,1536]{1,0:T(8,128)}, u32[]{:S(2)}) copy-start(f32[48,1536]{1,0:T(8,128)} %reduce-scatter.12.cloned.1.call-done) | copy-start | bytes 884740
  1327.3 71.8 %copy-start.31 = (f32[48,1536]{1,0:T(8,128)S(1)}, f32[48,1536]{1,0:T(8,128)}, u32[]{:S(2)}) copy-start(f32[48,1536]{1,0:T(8,128)} %param.33) | copy-start | bytes 884740
  1327.4 71.8 %copy-start.32 = (f32[48,1536]{1,0:T(8,128)S(1)}, f32[48,1536]{1,0:T(8,128)}, u32[]{:S(2)}) copy-start(f32[48,1536]{1,0:T(8,128)} %param.32) | copy-start | bytes 884740
  1327.4 72.8 %copy-start.25 = (f32[1536,48]{0,1:T(8,128)S(1)}, f32[1536,48]{0,1:T(8,128)}, u32[]{:S(2)}) copy-start(f32[1536,48]{0,1:T(8,128)} %param.26) | copy-start | bytes 884740
  1327.4 72.8 %copy-start.26 = (f32[1536,48]{0,1:T(8,128)S(1)}, f32[1536,48]{0,1:T(8,128)}, u32[]{:S(2)}) copy-start(f32[1536,48]{0,1:T(8,128)} %reduce-scatter.14.cloned.1.call-done) | copy-start | bytes 884740
  1327.4 72.8 %copy-start.33 = (f32[1536,48]{0,1:T(8,128)S(1)}, f32[1536,48]{0,1:T(8,128)}, u32[]{:S(2)}) copy-start(f32[1536,48]{0,1:T(8,128)} %param.35) | copy-start | bytes 884740
  1327.4 72.8 %copy-start.34 = (f32[1536,48]{0,1:T(8,128)S(1)}, f32[1536,48]{0,1:T(8,128)}, u32[]{:S(2)}) copy-start(f32[1536,48]{0,1:T(8,128)} %param.34) | copy-start | bytes 884740
  (47 other events, 897.1 us)
Sparse Core Ops, SparseCore 0:
  11.3 62.0 all-gather.5
  107.5 30.7 all-reduce.6
  142.1 63.4 all-gather.7
  209.2 61.0 all-gather.9
  320.9 30.8 all-reduce.8
  446.4 27.9 all-reduce.10
  524.6 33.1 all-reduce.12
  600.2 33.2 all-reduce.14
  648.6 122.7 reduce-scatter.15
  776.0 123.4 reduce-scatter.9
  904.6 137.1 reduce-scatter.13
  1047.6 136.5 reduce-scatter.11
  1189.3 133.6 reduce-scatter.7
  1325.2 22.4 all-reduce.16
where the time goes:
time: 1420 us; the launch traced here: 1410 us
  waiting for transfers between devices  853 us (60%)
  matrix products  218 us (15%)
  blocking collectives  169 us (12%)
  other arithmetic  86.9 us (6%)
  local copies, waits for them, and re-layouts  59.2 us (4%)
  between operations  23.8 us (2%)
    reduce_scatter x1, waiting for transfers between devices, backward_pass(): lax.psum_scatter(grad_up, 'dp', scatter_dimension=0, tiled=True)  141 us
    reduce_scatter x1, waiting for transfers between devices, backward_pass(): lax.psum_scatter(grad_down, 'dp', scatter_dimension=1, tiled=True)  141 us
    reduce_scatter x1, waiting for transfers between devices, backward_pass(): lax.psum_scatter(grad_qkv, 'dp', scatter_dimension=0, tiled=True)  137 us
    reduce_scatter x1, waiting for transfers between devices, backward_pass(): lax.psum_scatter(grad_proj, 'dp', scatter_dimension=1, tiled=True)  126 us
    psum x5, waiting for transfers between devices, tensor_total(): return lax.psum(partial_rows, 'tensor')  116 us
    all_gather x1, waiting for transfers between devices, body(): lax.all_gather(ffn_out_weight.astype(jnp.bfloat16), 'dp', axis=1, tiled=T...  64.7 us
    dot_general x2, matrix products, forward_pass(): ffn_part = jnp.dot(activated, ffn_out, preferred_element_type=jnp.float32)  57.4 us
    all_gather x1, waiting for transfers between devices, body(): lax.all_gather(ffn_in_weight.astype(jnp.bfloat16), 'dp', axis=0, tiled=True)  50.1 us
  transfers between devices with their start and end apart: 14, of which 13 were waited for; matrix products, arithmetic and copies ran while one was open for 7% of the time, Pallas kernels for 0%

commit v1 on v0

v1 whole, which is shorter than its diff:
```python
from functools import partial

import jax
import jax.numpy as jnp
from jax import lax
from jax.experimental import pallas as pl
from jax.experimental.pallas import tpu as pltpu
from jax.sharding import PartitionSpec as P

HEAD = 64
SPAN = 128
STEP = 10
D = 768
FF = 3072
NB = 16
RB = D // NB
HALF_QKV = 1152
HALF_OUT = 384
HALF_FF = 1536
ONE = HALF_QKV + HALF_OUT + 128
CONTRAST = 4.0
EPS = 1e-06
BF = jnp.bfloat16
F32 = jnp.float32
AXES = ("dp", "tensor")

NN = (((1,), (0,)), ((), ()))
NT = (((1,), (1,)), ((), ()))
TN = (((0,), (0,)), ((), ()))


def mm(left, right, dims=NN):
    return lax.dot_general(left, right, dims, preferred_element_type=F32)


def params(vmem=56):
    return pltpu.CompilerParams(vmem_limit_bytes=vmem * 2**20)


def cost(flops, bytes_accessed, trans=0):
    return pl.CostEstimate(flops=int(flops), bytes_accessed=int(bytes_accessed), transcendentals=int(trans))


HBM = pl.BlockSpec(memory_space=pl.ANY)


def bit_orders(n_dp):
    bits = n_dp.bit_length() - 1
    if bits == 4:
        return ((4, 8, 2, 1), (8, 4, 1, 2))
    up = tuple(1 << b for b in range(bits))[::-1]
    half = bits // 2
    return (up, up[: half - 1] + up[half - 1 :][::-1] if bits > 2 else up[::-1])


def pairs_of(n_dp, orders, step):
    out = []
    for d in range(n_dp):
        for c in range(2):
            out.append((d * 2 + c, (d ^ orders[c][step]) * 2 + c))
    return out


def rel_of(order):
    out = []
    for p in range(1 << len(order)):
        r = 0
        for k, b in enumerate(order):
            if (p >> k) & 1:
                r ^= b
        out.append(r)
    return out


def core_swap(block):
    return lax.ppermute(block, "tensor", [(0, 1), (1, 0)])


def gather_group(shard, n_dp):
    orders = bit_orders(n_dp)
    steps = len(orders[0])
    held = shard[None]
    for k in range(steps):
        came = lax.ppermute(held, AXES, pairs_of(n_dp, orders, k))
        if k == steps - 1:
            return held, came
        held = jnp.concatenate([held, came], axis=0)


def scatter_group(own, other, n_dp):
    orders = bit_orders(n_dp)
    steps = len(orders[0])
    size = n_dp // 2
    keep = own[:size].astype(F32) + other[:size].astype(F32)
    send = (own[size:].astype(F32) + other[size:].astype(F32)).astype(BF)
    keep = keep.astype(BF)
    for k in reversed(range(steps)):
        came = lax.ppermute(send, AXES, pairs_of(n_dp, orders, k))
        if k == 0:
            return keep[0].astype(F32) + came[0].astype(F32)
        size //= 2
        total = keep.astype(F32) + came.astype(F32)
        keep = total[:size].astype(BF)
        send = total[size:].astype(BF)


def load_pieces(refs, tab, dest, sems):
    copies = []
    core = tab[0]
    for n, ref in enumerate(refs):
        half = core if n < 2 else 1 - core
        for p in range(NB // 2):
            q = (n % 2) * (NB // 2) + p
            place = tab[2 + (n // 2) * NB + q]
            copies.append(pltpu.make_async_copy(ref.at[p], dest.at[half, place], sems.at[n * (NB // 2) + p]))
    for c in copies:
        c.start()
    for c in copies:
        c.wait()


def weight(scratch, half, first, last):
    return scratch[half, :, :, first:last].reshape(D, last - first)


def norm_fwd(hidden):
    center = hidden - jnp.mean(hidden, axis=-1, keepdims=True)
    spread = jnp.mean(center * center, axis=-1, keepdims=True)
    rstd = lax.rsqrt(spread + EPS)
    return center * rstd, rstd


def norm_bwd(grad, xh, rstd, gain):
    e = grad * gain
    m1 = jnp.mean(e, axis=-1, keepdims=True)
    m2 = jnp.mean(e * xh, axis=-1, keepdims=True)
    return rstd * (e - m1 - xh * m2)


def head_masks(rows, scale):
    lane = lax.broadcasted_iota(jnp.int32, (rows, 128), 1)
    return (
        jnp.where(lane < HEAD, scale, 0.0).astype(BF),
        jnp.where(lane < HEAD, 0.0, scale).astype(BF),
    )


def stack_heads(pair, masks):
    return jnp.concatenate([pair * masks[0], pair * masks[1]], axis=0)


def merge_heads(both):
    lane = lax.broadcasted_iota(jnp.int32, (SPAN, 128), 1)
    return jnp.where(lane < HEAD, both[:SPAN], both[SPAN:])


def attn_fwd_kernel(
    tab, tok_ref, w0, w1, w2, w3, qkv_ref, ctx_ref, lse_ref, xh_ref, rstd_ref, tokt_ref, p_ref, w, sems
):
    @pl.when(pl.program_id(0) == 0)
    def _():
        load_pieces((w0, w1, w2, w3), tab, w, sems)
        cols = weight(w, 0, HALF_QKV + HALF_OUT, ONE).astype(F32)
        p_ref[...] = cols.T[:8]

    x = tok_ref[...]
    tokt_ref[...] = x.T
    masks = head_masks(SPAN, HEAD ** (-0.5))
    attn = x.astype(F32)
    for h in range(2):
        qkv = mm(x, weight(w, h, 0, HALF_QKV)).astype(BF)
        qkv_ref[h] = qkv
        rows = []
        for s in range(2):
            own = qkv[s * SPAN : (s + 1) * SPAN]
            parts = []
            for j in range(3):
                q = stack_heads(own[:, j * 128 : (j + 1) * 128], masks)
                k = own[:, HALF_OUT + j * 128 : HALF_OUT + (j + 1) * 128]
                v = own[:, 2 * HALF_OUT + j * 128 : 2 * HALF_OUT + (j + 1) * 128]
                st = mm(k, q, NT)
                top = jnp.max(st, axis=0, keepdims=True)
                ex = jnp.exp(st - top)
                total = jnp.sum(ex, axis=0, keepdims=True)
                pt = (ex * (1.0 / total)).astype(BF)
                lse_ref[s, h * 3 + j : h * 3 + j + 1, :] = top + jnp.log(total)
                parts.append(merge_heads(mm(pt, v, TN)).astype(BF))
            rows.append(jnp.concatenate(parts, axis=1))
        ctx = jnp.concatenate(rows, axis=0)
        ctx_ref[h] = ctx
        attn = attn + mm(ctx, weight(w, h, HALF_QKV, HALF_QKV + HALF_OUT), NT)
    xh, rstd = norm_fwd(attn)
    rstd = jnp.broadcast_to(rstd, (2 * SPAN, 128))
    for s in range(2):
        for q in range(4):
            r = s * SPAN + q * 32
            xh_ref[q, s] = xh[r : r + 32]
            rstd_ref[q, s] = rstd[r : r + 32]


def attn_fwd(tab, tokens, pieces, rows):
    spans = rows // SPAN
    steps = spans // 2
    out = [
        jax.ShapeDtypeStruct((2, rows, HALF_QKV), BF),
        jax.ShapeDtypeStruct((2, rows, HALF_OUT), BF),
        jax.ShapeDtypeStruct((spans, 8, 2 * SPAN), F32),
        jax.ShapeDtypeStruct((4, spans, 32, D), F32),
        jax.ShapeDtypeStruct((4, spans, 32, 128), F32),
        jax.ShapeDtypeStruct((D, rows), BF),
        jax.ShapeDtypeStruct((8, D), F32),
    ]
    return pl.pallas_call(
        attn_fwd_kernel,
        out_shape=out,
        grid_spec=pltpu.PrefetchScalarGridSpec(
            num_scalar_prefetch=1,
            grid=(steps,),
            in_specs=[pl.BlockSpec((2 * SPAN, D), lambda i, tab: (tab[0] * steps + i, 0))] + [HBM] * 4,
            out_specs=[
                pl.BlockSpec((2, 2 * SPAN, HALF_QKV), lambda i, tab: (0, i, 0)),
                pl.BlockSpec((2, 2 * SPAN, HALF_OUT), lambda i, tab: (0, i, 0)),
                pl.BlockSpec((2, 8, 2 * SPAN), lambda i, tab: (i, 0, 0)),
                pl.BlockSpec((4, 2, 32, D), lambda i, tab: (0, i, 0, 0)),
                pl.BlockSpec((4, 2, 32, 128), lambda i, tab: (0, i, 0, 0)),
                pl.BlockSpec((D, 2 * SPAN), lambda i, tab: (0, i)),
                pl.BlockSpec((8, D), lambda i, tab: (0, 0)),
            ],
            scratch_shapes=[pltpu.VMEM((2, NB, RB, ONE), BF), pltpu.SemaphoreType.DMA((2 * NB,))],
        ),
        compiler_params=params(),
        cost_estimate=cost(rows * 8.2e6, rows * 20000 + 5e6, rows * 1600),
        name="attn_fwd",
    )(tab, tokens, *pieces)


def gelu_pair(u):
    a = jnp.abs(u)
    t = 1.0 / (1.0 + (0.3275911 * 0.5**0.5) * a)
    e = jnp.exp(-0.5 * u * u)
    poly = 1.061405429 * t - 1.453152027
    poly = poly * t + 1.421413741
    poly = poly * t - 0.284496736
    poly = poly * t + 0.254829592
    tail = (0.5 * poly * t) * e
    phi = jnp.where(u >= 0.0, 1.0 - tail, tail)
    return u * phi, phi + (0.3989422804014327 * u) * e


TILE = 512


def ffn_up_kernel(tab, xh_ref, p_ref, w0, w1, w2, w3, g_ref, gp_ref, yt_ref, w, sems):
    @pl.when(pl.program_id(0) == 0)
    def _():
        load_pieces((w0, w1, w2, w3), tab, w, sems)

    y = xh_ref[...] * p_ref[0:1, :] + p_ref[1:2, :]
    yb = y.astype(BF)
    yt_ref[...] = yb.T
    for h in range(2):
        for t in range(HALF_FF // TILE):
            u = mm(yb, weight(w, h, t * TILE, (t + 1) * TILE))
            g, gp = gelu_pair(u)
            g_ref[h, :, t * TILE : (t + 1) * TILE] = g.astype(BF)
            gp_ref[h, :, t * TILE : (t + 1) * TILE] = gp.astype(BF)


def ffn_up(tab, xh, prow, pieces, rows):
    steps = 4
    blk = rows // steps
    return pl.pallas_call(
        ffn_up_kernel,
        out_shape=[
            jax.ShapeDtypeStruct((2, rows, HALF_FF), BF),
            jax.ShapeDtypeStruct((2, rows, HALF_FF), BF),
            jax.ShapeDtypeStruct((D, rows), BF),
        ],
        grid_spec=pltpu.PrefetchScalarGridSpec(
            num_scalar_prefetch=1,
            grid=(steps,),
            in_specs=[
                pl.BlockSpec((blk, D), lambda i, tab: (i, 0)),
                pl.BlockSpec((8, D), lambda i, tab: (0, 0)),
            ]
            + [HBM] * 4,
            out_specs=[
                pl.BlockSpec((2, blk, HALF_FF), lambda i, tab: (0, i, 0)),
                pl.BlockSpec((2, blk, HALF_FF), lambda i, tab: (0, i, 0)),
                pl.BlockSpec((D, blk), lambda i, tab: (0, i)),
            ],
            scratch_shapes=[pltpu.VMEM((2, NB, RB, HALF_FF), BF), pltpu.SemaphoreType.DMA((2 * NB,))],
        ),
        compiler_params=params(),
        cost_estimate=cost(rows * 4.8e6, rows * 18000 + 5e6, rows * 6000),
        name="ffn_up",
    )(tab, xh, prow, *pieces)


def ffn_down_kernel(tab, xh1_ref, p_ref, g_ref, w0, w1, w2, w3, mixed_ref, cls_ref, xh_ref, rstd_ref, w, sems):
    @pl.when(pl.program_id(0) == 0)
    def _():
        load_pieces((w0, w1, w2, w3), tab, w, sems)

    total = xh1_ref[...] * p_ref[0:1, :] + p_ref[1:2, :]
    for h in range(2):
        total = total + mm(g_ref[h], weight(w, h, 0, HALF_FF), NT)
    xh, rstd = norm_fwd(total)
    xh_ref[...] = xh
    rstd_ref[...] = jnp.broadcast_to(rstd, rstd_ref.shape)
    out = xh * p_ref[2:3, :] + p_ref[3:4, :]
    mixed_ref[...] = out.astype(BF).reshape(mixed_ref.shape)

    @pl.when(pl.program_id(0) == 0)
    def _():
        cls_ref[...] = out.reshape(mixed_ref.shape)[:, 0, :]


def ffn_down(tab, xh1, prow, g, pieces, rows):
    steps = 4
    blk = rows // steps
    spans = rows // SPAN
    return pl.pallas_call(
        ffn_down_kernel,
        out_shape=[
            jax.ShapeDtypeStruct((spans, SPAN, D), BF),
            jax.ShapeDtypeStruct((spans, D), F32),
            jax.ShapeDtypeStruct((rows, D), F32),
            jax.ShapeDtypeStruct((rows, 128), F32),
        ],
        grid_spec=pltpu.PrefetchScalarGridSpec(
            num_scalar_prefetch=1,
            grid=(steps,),
            in_specs=[
                pl.BlockSpec((blk, D), lambda i, tab: (i, 0)),
                pl.BlockSpec((8, D), lambda i, tab: (0, 0)),
                pl.BlockSpec((2, blk, HALF_FF), lambda i, tab: (0, i, 0)),
            ]
            + [HBM] * 4,
            out_specs=[
                pl.BlockSpec((spans, 32, D), lambda i, tab: (0, i, 0)),
                pl.BlockSpec((spans, D), lambda i, tab: (0, 0)),
                pl.BlockSpec((blk, D), lambda i, tab: (i, 0)),
                pl.BlockSpec((blk, 128), lambda i, tab: (i, 0)),
            ],
            scratch_shapes=[pltpu.VMEM((2, NB, RB, HALF_FF), BF), pltpu.SemaphoreType.DMA((2 * NB,))],
        ),
        compiler_params=params(),
        cost_estimate=cost(rows * 4.8e6, rows * 16000 + 5e6, rows),
        name="ffn_down",
    )(tab, xh1, prow, g, *pieces)


def contrast_kernel(where, doc_row, doc_col, cls_ref, loss_ref, grad_ref, rows, own_doc):
    spans = doc_row.shape[1]
    blocks, per = cls_ref.shape[0], cls_ref.shape[1]
    me = where[0]
    for n in range(blocks):
        rows[where[1 + n]] = cls_ref[n].astype(F32)
    a = rows[...].reshape(spans, D).astype(BF)
    own = rows[me].astype(BF)
    scale = D ** (-0.5)
    col = lax.broadcasted_iota(jnp.int32, (spans, spans), 1)
    row = lax.broadcasted_iota(jnp.int32, (spans, spans), 0)
    logits = mm(a, a, NT) * scale
    partner = (doc_col[...] == doc_row[...]) & (row != col)
    masked = jnp.where(row == col, -1000000000.0, logits)
    top = jnp.max(masked, axis=0, keepdims=True)
    lse = jnp.log(jnp.sum(jnp.exp(masked - top), axis=0, keepdims=True)) + top
    positive = jnp.sum(jnp.where(partner, logits, 0.0), axis=0, keepdims=True)
    flagged = jnp.max(jnp.where(partner, 1.0, 0.0), axis=0, keepdims=True)
    count = jnp.sum(flagged, axis=1, keepdims=True)
    loss = jnp.sum(flagged * (lse - positive), axis=1, keepdims=True) / count
    loss_ref[...] = jnp.broadcast_to(loss, loss_ref.shape)

    weight_row = flagged * (CONTRAST * spans) / count
    own_doc[...] = doc_col[...].reshape(blocks, per, 1)
    docs = own_doc[me]
    col = lax.broadcasted_iota(jnp.int32, (per, spans), 1)
    row = lax.broadcasted_iota(jnp.int32, (per, spans), 0) + me * per
    logits = mm(own, a, NT) * scale
    same = jnp.where((docs == doc_row[...]) & (row != col), 1.0, 0.0)
    masked = jnp.where(row == col, -1000000000.0, logits)
    top = jnp.max(masked, axis=1, keepdims=True)
    ex = jnp.exp(masked - top)
    soft = ex / jnp.sum(ex, axis=1, keepdims=True)
    own_weight = jnp.max(same, axis=1, keepdims=True) * (CONTRAST * spans) / count
    sym = own_weight * (soft - same) + weight_row * (jnp.exp(masked - lse) - same)
    high = sym.astype(BF)
    low = (sym - high.astype(F32)).astype(BF)
    grad_ref[...] = (mm(high, a) + mm(low, a)) * scale


def contrast(where, span_doc, cls_all):
    blocks, per, _ = cls_all.shape
    spans = blocks * per
    vm = pl.BlockSpec(memory_space=pltpu.VMEM)
    return pl.pallas_call(
        contrast_kernel,
        out_shape=[jax.ShapeDtypeStruct((1, 128), F32), jax.ShapeDtypeStruct((per, D), F32)],
        in_specs=[pl.BlockSpec(memory_space=pltpu.SMEM), vm, vm, vm],
        out_specs=[vm, vm],
        scratch_shapes=[pltpu.VMEM((blocks, per, D), F32), pltpu.VMEM((blocks, per, 1), jnp.int32)],
        compiler_params=params(),
        name="contrast",
    )(where, span_doc.reshape(1, spans), span_doc.reshape(spans, 1), cls_all)


def norm_two_kernel(tab, cot_ref, cls_ref, xh_ref, rstd_ref, p_ref, dh_ref, dft_ref, sums_ref):
    i = pl.program_id(0)
    spans = cls_ref.shape[0]
    grad = cot_ref[...].astype(F32)
    first = lax.broadcasted_iota(jnp.int32, grad.shape, 1) == 0
    extra = jnp.where(jnp.logical_and(first, i == 0), cls_ref[...].reshape(spans, 1, D), 0.0)
    grad = (grad + extra).reshape(spans * 32, D)
    xh = xh_ref[...]
    dh = norm_bwd(grad, xh, rstd_ref[:, 0:1], p_ref[2:3, :])
    dh_ref[...] = dh
    dft_ref[...] = dh.astype(BF).T

    @pl.when(i == 0)
    def _():
        sums_ref[...] = jnp.zeros_like(sums_ref)

    sums_ref[0:1, :] += jnp.sum(grad * xh, axis=0, keepdims=True)
    sums_ref[1:2, :] += jnp.sum(grad, axis=0, keepdims=True)


def norm_two(tab, cotangent, grad_cls, xh, rstd, prow, rows):
    spans = rows // SPAN
    blk = rows // 4
    return pl.pallas_call(
        norm_two_kernel,
        out_shape=[
            jax.ShapeDtypeStruct((rows, D), F32),
            jax.ShapeDtypeStruct((D, rows), BF),
            jax.ShapeDtypeStruct((8, D), F32),
        ],
        grid_spec=pltpu.PrefetchScalarGridSpec(
            num_scalar_prefetch=1,
            grid=(4,),
            in_specs=[
                pl.BlockSpec((spans, 32, D), lambda i, tab: (tab[0], i, 0)),
                pl.BlockSpec((spans, D), lambda i, tab: (0, 0)),
                pl.BlockSpec((blk, D), lambda i, tab: (i, 0)),
                pl.BlockSpec((blk, 128), lambda i, tab: (i, 0)),
                pl.BlockSpec((8, D), lambda i, tab: (0, 0)),
            ],
            out_specs=[
                pl.BlockSpec((blk, D), lambda i, tab: (i, 0)),
                pl.BlockSpec((D, blk), lambda i, tab: (0, i)),
                pl.BlockSpec((8, D), lambda i, tab: (0, 0)),
            ],
        ),
        compiler_params=params(),
        cost_estimate=cost(rows * D * 20, rows * 12000, rows),
        name="norm_two",
    )(tab, cotangent.reshape(-1, SPAN, D), grad_cls, xh, rstd, prow)


def ffn_back_kernel(
    tab, dh_ref, gp_ref, xh1_ref, rstd1_ref, p_ref, u0, u1, u2, u3, d0, d1, d2, d3,
    du_ref, dh1_ref, sums_ref, wu, wd, sem_u, sem_d,
):
    i = pl.program_id(0)

    @pl.when(i == 0)
    def _():
        load_pieces((d0, d1, d2, d3), tab, wd, sem_d)
        load_pieces((u0, u1, u2, u3), tab, wu, sem_u)
        sums_ref[...] = jnp.zeros_like(sums_ref)

    dh = dh_ref[...]
    df = dh.astype(BF)
    grad = dh
    for h in range(2):
        for t in range(HALF_FF // TILE):
            lo, hi = t * TILE, (t + 1) * TILE
            dg = mm(df, weight(wd, h, lo, hi))
            du = (dg * gp_ref[h, :, lo:hi].astype(F32)).astype(BF)
            du_ref[h, :, lo:hi] = du
        grad = grad + mm(du_ref[h], weight(wu, h, 0, HALF_FF), NT)
    xh = xh1_ref[...]
    dh1_ref[...] = norm_bwd(grad, xh, rstd1_ref[:, 0:1], p_ref[0:1, :])
    sums_ref[0:1, :] += jnp.sum(grad * xh, axis=0, keepdims=True)
    sums_ref[1:2, :] += jnp.sum(grad, axis=0, keepdims=True)


def ffn_back(tab, dh2, gp, xh1, rstd1, prow, up, down, rows):
    steps = 4
    blk = rows // steps
    return pl.pallas_call(
        ffn_back_kernel,
        out_shape=[
            jax.ShapeDtypeStruct((2, rows, HALF_FF), BF),
            jax.ShapeDtypeStruct((rows, D), F32),
            jax.ShapeDtypeStruct((8, D), F32),
        ],
        grid_spec=pltpu.PrefetchScalarGridSpec(
            num_scalar_prefetch=1,
            grid=(steps,),
            in_specs=[
                pl.BlockSpec((blk, D), lambda i, tab: (i, 0)),
                pl.BlockSpec((2, blk, HALF_FF), lambda i, tab: (0, i, 0)),
                pl.BlockSpec((blk, D), lambda i, tab: (i, 0)),
                pl.BlockSpec((blk, 128), lambda i, tab: (i, 0)),
                pl.BlockSpec((8, D), lambda i, tab: (0, 0)),
            ]
            + [HBM] * 8,
            out_specs=[
                pl.BlockSpec((2, blk, HALF_FF), lambda i, tab: (0, i, 0)),
                pl.BlockSpec((blk, D), lambda i, tab: (i, 0)),
                pl.BlockSpec((8, D), lambda i, tab: (0, 0)),
            ],
            scratch_shapes=[
                pltpu.VMEM((2, NB, RB, HALF_FF), BF),
                pltpu.VMEM((2, NB, RB, HALF_FF), BF),
                pltpu.SemaphoreType.DMA((2 * NB,)),
                pltpu.SemaphoreType.DMA((2 * NB,)),
            ],
        ),
        compiler_params=params(),
        cost_estimate=cost(rows * 9.5e6, rows * 24000 + 1e7, rows),
        name="ffn_back",
    )(tab, dh2, gp, xh1, rstd1, prow, *up, *down)


def store_blocks(out_ref, grad, tab, first):
    for j in range(NB):
        out_ref[tab[first + j]] = grad[j * RB : (j + 1) * RB].astype(BF)


def weight_grad_kernel(tab, xt_ref, y_ref, out_ref):
    store_blocks(out_ref, mm(xt_ref[...], y_ref[...]), tab, 1)


def weight_grad(tab, xt, y, name):
    rows = xt.shape[1]
    width = y.shape[2]
    tile = 512
    return pl.pallas_call(
        weight_grad_kernel,
        out_shape=jax.ShapeDtypeStruct((NB, RB, width), BF),
        grid_spec=pltpu.PrefetchScalarGridSpec(
            num_scalar_prefetch=1,
            grid=(width // tile,),
            in_specs=[
                pl.BlockSpec((D, rows), lambda t, tab: (0, 0)),
                pl.BlockSpec((None, rows, tile), lambda t, tab: (tab[0], 0, t)),
            ],
            out_specs=pl.BlockSpec((NB, RB, tile), lambda t, tab: (0, 0, t)),
        ),
        compiler_params=params(),
        cost_estimate=cost(2 * rows * D * width, rows * (D + width) * 2 + D * width * 2),
        name=name,
    )(tab, xt, y)


def attn_back_kernel(
    tab, dh1_ref, qkv_ref, lse_ref, w0, w1, w2, w3, dqkv_ref, dat_ref, dh1n_ref, w, sems
):
    @pl.when(pl.program_id(0) == 0)
    def _():
        load_pieces((w0, w1, w2, w3), tab, w, sems)

    dh1 = jnp.concatenate([dh1_ref[q, s] for s in range(2) for q in range(4)], axis=0)
    dh1n_ref[...] = dh1
    da = dh1.astype(BF)
    dat_ref[...] = da.T
    masks = head_masks(SPAN, HEAD ** (-0.5))
    plain = head_masks(SPAN, 1.0)
    for h in range(2):
        dctx = mm(da, weight(w, h, HALF_QKV, HALF_QKV + HALF_OUT)).astype(BF)
        for s in range(2):
            lo, hi = s * SPAN, (s + 1) * SPAN
            for j in range(3):
                a, b = j * 128, (j + 1) * 128
                q = stack_heads(qkv_ref[h, lo:hi, a:b], masks)
                k = qkv_ref[h, lo:hi, HALF_OUT + a : HALF_OUT + b]
                v = qkv_ref[h, lo:hi, 2 * HALF_OUT + a : 2 * HALF_OUT + b]
                dc = stack_heads(dctx[lo:hi, a:b], plain)
                st = mm(k, q, NT)
                pt = jnp.exp(st - lse_ref[s, h * 3 + j : h * 3 + j + 1, :])
                dpt = mm(v, dc, NT)
                dst = pt * (dpt - jnp.sum(pt * dpt, axis=0, keepdims=True))
                dst = dst.astype(BF)
                dv = mm(pt.astype(BF), dc)
                dk = mm(dst, q)
                dq = merge_heads(mm(dst, k, TN)) * HEAD ** (-0.5)
                dqkv_ref[h, lo:hi, a:b] = dq.astype(BF)
                dqkv_ref[h, lo:hi, HALF_OUT + a : HALF_OUT + b] = dk.astype(BF)
                dqkv_ref[h, lo:hi, 2 * HALF_OUT + a : 2 * HALF_OUT + b] = dv.astype(BF)


def attn_back(tab, dh1, qkv, lse, pieces, rows):
    spans = rows // SPAN
    steps = spans // 2
    return pl.pallas_call(
        attn_back_kernel,
        out_shape=[
            jax.ShapeDtypeStruct((2, rows, HALF_QKV), BF),
            jax.ShapeDtypeStruct((D, rows), BF),
            jax.ShapeDtypeStruct((rows, D), F32),
        ],
        grid_spec=pltpu.PrefetchScalarGridSpec(
            num_scalar_prefetch=1,
            grid=(steps,),
            in_specs=[
                pl.BlockSpec((4, 2, 32, D), lambda i, tab: (0, i, 0, 0)),
                pl.BlockSpec((2, 2 * SPAN, HALF_QKV), lambda i, tab: (0, i, 0)),
                pl.BlockSpec((2, 8, 2 * SPAN), lambda i, tab: (i, 0, 0)),
            ]
            + [HBM] * 4,
            out_specs=[
                pl.BlockSpec((2, 2 * SPAN, HALF_QKV), lambda i, tab: (0, i, 0)),
                pl.BlockSpec((D, 2 * SPAN), lambda i, tab: (0, i)),
                pl.BlockSpec((2 * SPAN, D), lambda i, tab: (i, 0)),
            ],
            scratch_shapes=[pltpu.VMEM((2, NB, RB, ONE), BF), pltpu.SemaphoreType.DMA((2 * NB,))],
        ),
        compiler_params=params(),
        cost_estimate=cost(rows * 12e6, rows * 20000 + 5e6, rows * 1600),
        name="attn_back",
    )(tab, dh1.reshape(4, spans, 32, D), qkv, lse, *pieces)


def last_grad_kernel(tab, tokt_ref, dqkv_ref, dat_ref, ctx_ref, one_ref, two_ref, out_ref):
    t = pl.program_id(0)
    grad = mm(tokt_ref[...], dqkv_ref[...])
    for part in range(3):

        @pl.when(t == part)
        def _():
            for j in range(NB):
                out_ref[tab[1 + j], :, part * HALF_OUT : (part + 1) * HALF_OUT] = grad[
                    j * RB : (j + 1) * RB
                ].astype(BF)

    @pl.when(t == 2)
    def _():
        proj = mm(dat_ref[...], ctx_ref[...])
        norm = jnp.concatenate([one_ref[0:2, :], two_ref[0:2, :], jnp.zeros((124, D), F32)], axis=0).T
        for j in range(NB):
            out_ref[tab[1 + j], :, HALF_QKV : HALF_QKV + HALF_OUT] = proj[j * RB : (j + 1) * RB].astype(BF)
            out_ref[tab[1 + j], :, HALF_QKV + HALF_OUT : ONE] = norm[j * RB : (j + 1) * RB].astype(BF)


def last_grad(tab, tokt, dqkv, dat, ctx, one, two, name):
    rows = tokt.shape[1]
    return pl.pallas_call(
        last_grad_kernel,
        out_shape=jax.ShapeDtypeStruct((NB, RB, ONE), BF),
        grid_spec=pltpu.PrefetchScalarGridSpec(
            num_scalar_prefetch=1,
            grid=(3,),
            in_specs=[
                pl.BlockSpec((D, rows), lambda t, tab: (0, 0)),
                pl.BlockSpec((None, rows, HALF_OUT), lambda t, tab: (tab[0], 0, t)),
                pl.BlockSpec((D, rows), lambda t, tab: (0, 0)),
                pl.BlockSpec((None, rows, HALF_OUT), lambda t, tab: (tab[0], 0, 0)),
                pl.BlockSpec((8, D), lambda t, tab: (0, 0)),
                pl.BlockSpec((8, D), lambda t, tab: (0, 0)),
            ],
            out_specs=pl.BlockSpec((NB, RB, ONE), lambda t, tab: (0, 0, 0)),
        ),
        compiler_params=params(),
        cost_estimate=cost(2 * rows * D * ONE, rows * (D + ONE) * 4 + D * ONE * 2),
        name=name,
    )(tab, tokt, dqkv, dat, ctx, one, two)


def input_grad_kernel(tab, dh1_ref, dqkv_ref, w0, w1, w2, w3, out_ref, w, sems):
    @pl.when(pl.program_id(0) == 0)
    def _():
        load_pieces((w0, w1, w2, w3), tab, w, sems)

    total = dh1_ref[...]
    for h in range(2):
        total = total + mm(dqkv_ref[h], weight(w, h, 0, HALF_QKV), NT)
    out_ref[...] = total


def input_grads(tab, dh1, dqkv, pieces, rows):
    blk = 2 * SPAN
    return pl.pallas_call(
        input_grad_kernel,
        out_shape=jax.ShapeDtypeStruct((rows, D), F32),
        grid_spec=pltpu.PrefetchScalarGridSpec(
            num_scalar_prefetch=1,
            grid=(rows // blk,),
            in_specs=[
                pl.BlockSpec((blk, D), lambda i, tab: (i, 0)),
                pl.BlockSpec((2, blk, HALF_QKV), lambda i, tab: (0, i, 0)),
            ]
            + [HBM] * 4,
            out_specs=pl.BlockSpec((blk, D), lambda i, tab: (i, 0)),
            scratch_shapes=[pltpu.VMEM((2, NB, RB, ONE), BF), pltpu.SemaphoreType.DMA((2 * NB,))],
        ),
        compiler_params=params(),
        cost_estimate=cost(rows * 3.6e6, rows * 12000 + 5e6),
        name="input_grads",
    )(tab, dh1, dqkv, *pieces)


def adam_update(weight, gradient, moment_one, moment_two, step_rate, decay_rate):
    first_new = 0.9 * moment_one + 0.1 * gradient
    second_new = 0.999 * moment_two + 0.001 * gradient * gradient
    corr_first = first_new / (1.0 - 0.9**STEP)
    corr_second = second_new / (1.0 - 0.999**STEP)
    weight_new = weight - step_rate * (
        corr_first / (jnp.sqrt(corr_second) + 1e-08) + decay_rate * weight
    )
    return (first_new, second_new, weight_new)


def both_halves(own, core):
    other = core_swap(own)
    low = jnp.where(core == 0, own, other)
    high = jnp.where(core == 0, other, own)
    return jnp.concatenate([low, high], axis=0)


def body(
    tokens,
    cotangent,
    span_doc,
    qkv_weight,
    out_weight,
    ffn_in_weight,
    ffn_out_weight,
    norm_params,
    qkv_first,
    qkv_second,
    out_first,
    out_second,
    ffn_in_first,
    ffn_in_second,
    ffn_out_first,
    ffn_out_second,
    norm_first,
    norm_second,
):
    n_dp = lax.axis_size("dp")
    dp = lax.axis_index("dp")
    core = lax.axis_index("tensor")
    shard = D // n_dp
    rows = tokens.shape[0] // 2
    spans = rows // SPAN
    direct = n_dp == NB

    orders = bit_orders(n_dp)
    rel = jnp.array([rel_of(orders[0]), rel_of(orders[1])], jnp.int32)
    own_place = dp ^ rel[core]
    other_place = dp ^ rel[1 - core]
    if direct:
        head = jnp.stack([core, dp]).astype(jnp.int32)
        tab = jnp.concatenate([head, own_place, other_place]).astype(jnp.int32)
        back_own = jnp.argsort(own_place).astype(jnp.int32)
        back_other = jnp.argsort(other_place).astype(jnp.int32)
    else:
        plain = jnp.arange(NB, dtype=jnp.int32)
        head = jnp.stack([core, dp]).astype(jnp.int32)
        tab = jnp.concatenate([head, plain, plain]).astype(jnp.int32)
        back_own = back_other = plain
    tab_own = jnp.concatenate([core[None], back_own]).astype(jnp.int32)
    tab_other = jnp.concatenate([1 - core[None], back_other]).astype(jnp.int32)

    def gather(group):
        low, high = gather_group(group, n_dp)
        if direct:
            return low, high, core_swap(low), core_swap(high)
        full = jnp.concatenate([low, high], axis=0)
        full = full[jnp.argsort(own_place)].reshape(NB, RB, -1)
        other = core_swap(full)
        return full[: NB // 2], full[NB // 2 :], other[: NB // 2], other[NB // 2 :]

    def scatter(own, other):
        if not direct:
            own = own.reshape(n_dp, shard, -1)[own_place]
            other = other.reshape(n_dp, shard, -1)[other_place]
        return scatter_group(own, core_swap(other), n_dp)

    norm_cols = jnp.pad(norm_params.astype(BF).T, ((0, 0), (0, 124)))
    qkv_low = jnp.concatenate([qkv_weight[:, n].astype(BF) for n in range(3)], axis=1)
    group_one = jnp.concatenate([qkv_low, out_weight.T.astype(BF), norm_cols], axis=1)
    one = gather(group_one)
    up = gather(ffn_in_weight.astype(BF))
    down = gather(ffn_out_weight.T.astype(BF))

    qkv, ctx, lse, xh1, rstd1, tokt, prow = attn_fwd(tab, tokens, one, rows)
    xh1 = xh1.reshape(rows, D)
    rstd1 = rstd1.reshape(rows, 128)
    act, act_grad, yt = ffn_up(tab, xh1, prow, up, rows)
    mixed_own, cls_own, xh2, rstd2 = ffn_down(tab, xh1, prow, act, down, rows)

    held = cls_own.astype(BF)[None]
    order = ("tensor",) + tuple(1 << b for b in range(n_dp.bit_length() - 1))
    for step in order:
        if step == "tensor":
            came = core_swap(held)
        else:
            came = lax.ppermute(held, "dp", [(d, d ^ step) for d in range(n_dp)])
        held = jnp.concatenate([held, came], axis=0)
    me = dp * 2 + core
    where = jnp.concatenate([me[None], me ^ jnp.arange(2 * n_dp, dtype=jnp.int32)]).astype(jnp.int32)
    loss, grad_cls = contrast(where, span_doc, held)

    dh2, dft, two_sums = norm_two(tab, cotangent, grad_cls, xh2, rstd2, prow, rows)
    down_other = weight_grad(tab_other, dft, act, "down_other")
    down_own = weight_grad(tab_own, dft, act, "down_own")
    shard_down = scatter(down_own, down_other)
    du, dh1, one_sums = ffn_back(tab, dh2, act_grad, xh1, rstd1, prow, up, down, rows)
    up_other = weight_grad(tab_other, yt, du, "up_other")
    up_own = weight_grad(tab_own, yt, du, "up_own")
    shard_up = scatter(up_own, up_other)
    dqkv, dat, dh1 = attn_back(tab, dh1, qkv, lse, one, rows)
    last_other = last_grad(tab_other, tokt, dqkv, dat, ctx, one_sums, two_sums, "last_other")
    last_own = last_grad(tab_own, tokt, dqkv, dat, ctx, one_sums, two_sums, "last_own")
    shard_last = scatter(last_own, last_other)
    grad_in = input_grads(tab, dh1, dqkv, one, rows)

    mixed = both_halves(mixed_own.reshape(rows, D), core)
    input_grad = both_halves(grad_in, core)

    shard_qkv = shard_last[:, :HALF_QKV]
    shard_out = shard_last[:, HALF_QKV : HALF_QKV + HALF_OUT]
    shard_norm = shard_last[:, HALF_QKV + HALF_OUT : HALF_QKV + HALF_OUT + 4]
    shard_norm = (0.5 * (shard_norm + core_swap(shard_norm))).T
    squares = jnp.sum(shard_qkv * shard_qkv) + jnp.sum(shard_out * shard_out)
    squares = squares + jnp.sum(shard_up * shard_up) + jnp.sum(shard_down * shard_down)
    squares = squares + 0.5 * jnp.sum(shard_norm * shard_norm)
    squares = squares.reshape(1, 1)
    for step in order:
        if step == "tensor":
            squares = squares + core_swap(squares)
        else:
            squares = squares + lax.ppermute(squares, "dp", [(d, d ^ step) for d in range(n_dp)])
    clip_norm = jnp.sqrt(squares[0, 0])
    clip_scale = 1.0 / jnp.maximum(clip_norm, 1.0)
    grad_qkv = shard_qkv.reshape(shard, 3, HALF_OUT)
    qkv_new = adam_update(qkv_weight, grad_qkv * clip_scale, qkv_first, qkv_second, 0.02, 0.01)
    out_new = adam_update(out_weight, shard_out.T * clip_scale, out_first, out_second, 0.02, 0.01)
    up_new = adam_update(ffn_in_weight, shard_up * clip_scale, ffn_in_first, ffn_in_second, 0.02, 0.01)
    down_new = adam_update(
        ffn_out_weight, shard_down.T * clip_scale, ffn_out_first, ffn_out_second, 0.02, 0.01
    )
    norm_new = adam_update(norm_params, shard_norm * clip_scale, norm_first, norm_second, 0.5, 0.0)
    return (
        mixed,
        input_grad,
        loss[0, 0],
        clip_norm,
        *qkv_new,
        *out_new,
        *up_new,
        *down_new,
        *norm_new,
    )


def solution(mesh):
    rows = P("dp", None)
    qkv = P("dp", None, "tensor")
    turned = P("tensor", "dp")
    up = P("dp", "tensor")
    norm = P(None, "dp")
    weights = (qkv, turned, up, turned, norm)
    moments = tuple(spec for spec in weights for _ in range(2))
    updated = tuple(spec for spec in weights for _ in range(3))
    return jax.shard_map(
        body,
        mesh=mesh,
        in_specs=(rows, rows, P()) + weights + moments,
        out_specs=(rows, rows, P(), P()) + updated,
        check_vma=False,
    )
```

time: 1420 us -> 424 us (0.30)
  waiting for transfers between devices: 853 us -> 142 us
  matrix products: 218 us -> 0 us
  blocking collectives: 169 us -> 0 us
  Pallas kernels: 0 us -> 161 us
  starting transfers between devices: 1.37 us -> 65.6 us
  local copies, waits for them, and re-layouts: 59.2 us -> 6.91 us
  other arithmetic: 86.9 us -> 38.8 us
  between operations: 23.8 us -> 8.46 us
    reduce_scatter x4 -> x0, waiting for transfers between devices: 545 us -> none  [the longest x1 141 us: backward_pass(): lax.psum_scatter(grad_up, 'dp', scatter_dimension=0, tiled=True)]
    dot_general x25 -> x0, matrix products: 218 us -> none  [the longest x2 57.4 us: forward_pass(): ffn_part = jnp.dot(activated, ffn_out, preferred_element_type=jnp.float32)]
    pallas_call x0 -> x14, Pallas kernels: none -> 161 us  [the longest x4 27.4 us: weight_grad(): pl.pallas_call(weight_grad_kernel, out_shape=jax.ShapeDtypeStruct((NB, RB...]
    ppermute x0 -> x46, waiting for transfers between devices: none -> 142 us  [the longest x12 67.6 us: scatter_group(): came = lax.ppermute(send, AXES, pairs_of(n_dp, orders, k))]
    psum x6 -> x0, waiting for transfers between devices: 136 us -> none  [the longest x5 116 us: tensor_total(): return lax.psum(partial_rows, 'tensor')]
    all_gather x3 -> x0, waiting for transfers between devices: 132 us -> none  [the longest x1 64.7 us: body(): lax.all_gather(ffn_out_weight.astype(jnp.bfloat16), 'dp', axis=1, tiled=T...]
    all_gather x3 -> x0, blocking collectives: 129 us -> none  [the longest x1 46.9 us: body(): lax.all_gather(out_weight.astype(jnp.bfloat16), 'dp', axis=1, tiled=True)]
    ppermute x0 -> x46, starting transfers between devices: none -> 65.6 us  [the longest x12 27.9 us: gather_group(): came = lax.ppermute(held, AXES, pairs_of(n_dp, orders, k))]
  transfers between devices with their start and end apart: 14 -> 46, of which waited for: 13 -> 26; matrix products, arithmetic and copies ran while one was open for 7% -> 7% of each run, Pallas kernels for 0% -> 35%
where the time goes in v1:
time: 424 us; the launch traced here: 423 us
  Pallas kernels  161 us (38%)
  waiting for transfers between devices  142 us (33%)
  starting transfers between devices  65.6 us (15%)
  other arithmetic  38.8 us (9%)
  between operations  8.46 us (2%)
  local copies, waits for them, and re-layouts  6.91 us (2%)
    ppermute x12, waiting for transfers between devices, scatter_group(): came = lax.ppermute(send, AXES, pairs_of(n_dp, orders, k))  67.6 us
    ppermute x12, waiting for transfers between devices, gather_group(): came = lax.ppermute(held, AXES, pairs_of(n_dp, orders, k))  50.4 us
    ppermute x12, starting transfers between devices, gather_group(): came = lax.ppermute(held, AXES, pairs_of(n_dp, orders, k))  27.9 us
    pallas_call x4, Pallas kernels, weight_grad(): pl.pallas_call(weight_grad_kernel, out_shape=jax.ShapeDtypeStruct((NB, RB...  27.4 us
    pallas_call x1, Pallas kernels, ffn_back(): pl.pallas_call(ffn_back_kernel, out_shape=[jax.ShapeDtypeStruct((2, rows,...  21.4 us
    pallas_call x1, Pallas kernels, attn_back(): pl.pallas_call(attn_back_kernel, out_shape=[jax.ShapeDtypeStruct((2, rows...  21.4 us
    pallas_call x1, Pallas kernels, ffn_up(): pl.pallas_call(ffn_up_kernel, out_shape=[jax.ShapeDtypeStruct((2, rows, H...  21 us
    pallas_call x1, Pallas kernels, attn_fwd(): pl.pallas_call(attn_fwd_kernel, out_shape=out, grid_spec=pltpu.PrefetchSc...  18.2 us
  transfers between devices with their start and end apart: 46, of which 26 were waited for; matrix products, arithmetic and copies ran while one was open for 7% of the time, Pallas kernels for 35%

profile of v1, /device:TPU:0, one launch (start us, length us, event | category | flops | bytes accessed | tf_op | source)
XLA Modules:
  0.0 422.7 jit_solution(8044198621559263596)
XLA Ops:
  6.5 4.6 %collective-permute-done = bf16[1,48,1664]{2,1,0:T(8,128)(2,1)S(1)} collective-permute-done((bf16[1,48,1664]{2,1,0:T(8,128)(2,1)S(1)}, bf16[1,48,1664]{2,1,0:T(8,128)(2,1)S(1)}, u32[]{:S(2)}, u32[]{:S(2)}) %collective-permute-start) | collective-permute-done | bytes 159776 | tf_op jit(solution)/shard_map/ppermute | solution.py:84
  17.1 8.6 %collective-permute-done.1 = bf16[2,48,1664]{2,1,0:T(8,128)(2,1)S(1)} collective-permute-done((bf16[2,48,1664]{2,1,0:T(8,128)(2,1)S(1)}, bf16[2,48,1664]{2,1,0:T(8,128)(2,1)S(1)}, u32[]{:S(2)}, u32[]{:S(2)}) %collective-permute-start.1) | collective-permute-done | bytes 319520 | tf_op jit(solution)/shard_map/ppermute | solution.py:84
  49.4 11.5 %collective-permute-done.8 = bf16[4,48,1536]{2,1,0:T(8,128)(2,1)S(1)} collective-permute-done((bf16[4,48,1536]{2,1,0:T(8,128)(2,1)S(1)}, bf16[4,48,1536]{2,1,0:T(8,128)(2,1)S(1)}, u32[]{:S(2)}, u32[]{:S(2)}) %collective-permute-start.8) | collective-permute-done | bytes 589856 | tf_op jit(solution)/shard_map/ppermute | solution.py:84
  62.6 10.8 %collective-permute-done.14 = bf16[4,48,1536]{2,1,0:T(8,128)(2,1)S(1)} collective-permute-done((bf16[4,48,1536]{2,1,0:T(8,128)(2,1)S(1)}, bf16[4,48,1536]{2,1,0:T(8,128)(2,1)S(1)}, u32[]{:S(2)}, u32[]{:S(2)}) %collective-permute-start.14) | collective-permute-done | bytes 589856 | tf_op jit(solution)/shard_map/ppermute | solution.py:84
  83.0 8.2 %collective-permute-done.15.w1.d1 = bf16[8,48,1536]{2,1,0:T(8,128)(2,1)} collective-permute-done((bf16[8,48,1536]{2,1,0:T(8,128)(2,1)}, bf16[8,48,1536]{2,1,0:T(8,128)(2,1)}, u32[]{:S(2)}, u32[]{:S(2)}) %collective-permute-start.15) | collective-permute-done | bytes 1179680 | tf_op jit(solution)/shard_map/ppermute | solution.py:84
  91.7 18.2 %attn_fwd.1 = (bf16[2,1024,1152]{2,1,0:T(8,128)(2,1)}, bf16[2,1024,384]{2,1,0:T(8,128)(2,1)}, f32[8,8,256]{2,1,0:T(8,128)}, f32[4,8,32,768]{3,2,1,0:T(8,128)}, f...) custom-call(s32[34]{0:T(128)} %pad_add_fusion.tab, bf16[2048,768]{1,0:T(8,128)(2,1)} %tok_ref.1, ...), custom_call_target="tpu_custom_call" | custom-call | flops 8396800000 | bytes 25480000 | tf_op jit(solution)/shard_map/attn_fwd/pallas_call | solution.py:213
  110.0 21.0 %ffn_up.1 = (bf16[2,1024,1536]{2,1,0:T(8,128)(2,1)}, bf16[2,1024,1536]{2,1,0:T(8,128)(2,1)}, bf16[768,1024]{1,0:T(8,128)(2,1)}) custom-call(s32[34]{0:T(128)} %pad_add_fusion.tab, f32[1024,768]{1,0:T(8,128)} %bitcast.96, f32[8,768]{1,0:T(8,128)} %get-tuple-element.47.p_ref, bf16[8,48,1536]{2,1,0:T(8,128)(2,1)} %pad_maximum_fusion.3.w0.u0, ...), custom_call_target="tpu_custom_call" | custom-call | flops 4915200000 | bytes 23432000 | tf_op jit(solution)/shard_map/ffn_up/pallas_call | solution.py:272
  132.4 13.5 %ffn_down.1 = (bf16[8,128,768]{2,1,0:T(8,128)(2,1)}, f32[8,768]{1,0:T(8,128)}, f32[1024,768]{1,0:T(8,128)}, f32[1024,128]{1,0:T(8,128)}) custom-call(s32[34]{0:T(128)} %pad_add_fusion.tab, f32[1024,768]{1,0:T(8,128)} %bitcast.97, f32[8,768]{1,0:T(8,128)} %get-tuple-element.47.p_ref, bf16[2,1024,1536]{2,1,0:T(8,128)(2,1)} %get-tuple-element.48.g_ref.y_ref, ...), custom_call_target="tpu_custom_call" | custom-call | flops 4915200000 | bytes 21384000 | tf_op jit(solution)/shard_map/ffn_down/pallas_call | solution.py:323
  166.9 5.9 %collective-permute-done.23 = bf16[16,8,768]{2,1,0:T(8,128)(2,1)S(1)} collective-permute-done((bf16[16,8,768]{2,1,0:T(8,128)(2,1)S(1)}, bf16[16,8,768]{2,1,0:T(8,128)(2,1)S(1)}, u32[]{:S(2)}, u32[]{:S(2)}) %collective-permute-start.23) | collective-permute-done | bytes 196640 | tf_op jit(solution)/shard_map/ppermute | solution.py:802
  176.0 6.7 %norm_two.1 = (f32[1024,768]{1,0:T(8,128)}, bf16[768,1024]{1,0:T(8,128)(2,1)}, f32[8,768]{1,0:T(8,128)}) custom-call(s32[34]{0:T(128)} %pad_add_fusion.tab, bf16[16,128,768]{2,1,0:T(8,128)(2,1)} %bitcast.85, f32[8,768]{1,0:T(8,128)} %get-tuple-element.51.cls_ref, f32[1024,768]{1,0:T(8,128)} %get-tuple-element.52.xh_ref, ...), custom_call_target="tpu_custom_call" | custom-call | flops 15728640 | bytes 12288000 | tf_op jit(solution)/shard_map/norm_two/pallas_call | solution.py:432
  182.8 6.9 %down_other.1 = bf16[16,48,1536]{2,1,0:T(8,128)(2,1)} custom-call(s32[17]{0:T(128)} %pad_add_fusion.3.tab, bf16[768,1024]{1,0:T(8,128)(2,1)} %get-tuple-element.72.xt_ref, bf16[2,1024,1536]{2,1,0:T(8,128)(2,1)} %get-tuple-element.48.g_ref.y_ref), custom_call_target="tpu_custom_call" | custom-call | flops 2415919104 | bytes 7077888 | tf_op jit(solution)/shard_map/down_other/pallas_call | solution.py:541
  189.6 21.4 %ffn_back.1 = (bf16[2,1024,1536]{2,1,0:T(8,128)(2,1)}, f32[1024,768]{1,0:T(8,128)}, f32[8,768]{1,0:T(8,128)}) custom-call(s32[34]{0:T(128)} %pad_add_fusion.tab, f32[1024,768]{1,0:T(8,128)} %get-tuple-element.54.dh_ref, bf16[2,1024,1536]{2,1,0:T(8,128)(2,1)} %get-tuple-element.55.gp_ref, f32[1024,768]{1,0:T(8,128)} %bitcast.98, f32[1024,128]{1,0:T(8,128)} %bitcast.100, ...), custom_call_target="tpu_custom_call" | custom-call | flops 9728000000 | bytes 34576000 | tf_op jit(solution)/shard_map/ffn_back/pallas_call | solution.py:492
  211.1 21.4 %attn_back.1 = (bf16[2,1024,1152]{2,1,0:T(8,128)(2,1)}, bf16[768,1024]{1,0:T(8,128)(2,1)}, f32[1024,768]{1,0:T(8,128)}) custom-call(s32[34]{0:T(128)} %pad_add_fusion.tab, f32[4,8,32,768]{3,2,1,0:T(8,128)} %bitcast.99, bf16[2,1024,1152]{2,1,0:T(8,128)(2,1)} %get-tuple-element.58.qkv_ref, f32[8,8,256]{2,1,0:T(8,128)} %get-tuple-element.59.lse_ref, ...), custom_call_target="tpu_custom_call" | custom-call | flops 12288000000 | bytes 25480000 | tf_op jit(solution)/shard_map/attn_back/pallas_call | solution.py:598
  232.5 8.7 %last_other.1 = bf16[16,48,1664]{2,1,0:T(8,128)(2,1)} custom-call(s32[17]{0:T(128)} %pad_add_fusion.3.tab, bf16[768,1024]{1,0:T(8,128)(2,1)} %get-tuple-element.64.tokt_ref, bf16[2,1024,1152]{2,1,0:T(8,128)(2,1)} %get-tuple-element.61.dqkv_ref, bf16[768,1024]{1,0:T(8,128)(2,1)} %get-tuple-element.65.dat_ref, ...), custom_call_target="tpu_custom_call" | custom-call | flops 2617245696 | bytes 12517376 | tf_op jit(solution)/shard_map/last_other/pallas_call | solution.py:650
  241.7 6.8 %up_other.1 = bf16[16,48,1536]{2,1,0:T(8,128)(2,1)} custom-call(s32[17]{0:T(128)} %pad_add_fusion.3.tab, bf16[768,1024]{1,0:T(8,128)(2,1)} %get-tuple-element.70.xt_ref, bf16[2,1024,1536]{2,1,0:T(8,128)(2,1)} %get-tuple-element.71.y_ref), custom_call_target="tpu_custom_call" | custom-call | flops 2415919104 | bytes 7077888 | tf_op jit(solution)/shard_map/up_other/pallas_call | solution.py:541
  248.5 11.6 %input_grads.1 = f32[1024,768]{1,0:T(8,128)} custom-call(s32[34]{0:T(128)} %pad_add_fusion.tab, f32[1024,768]{1,0:T(8,128)} %get-tuple-element.60.dh1_ref, bf16[2,1024,1152]{2,1,0:T(8,128)(2,1)} %get-tuple-element.61.dqkv_ref, bf16[8,48,1664]{2,1,0:T(8,128)(2,1)} %copy-done.4, bf16[8,48,1664]{2,1,0:T(8,128)(2,1)} %copy-done.6, ...), custom_call_target="tpu_custom_call" | custom-call | flops 3686400000 | bytes 17288000 | tf_op jit(solution)/shard_map/input_grads/pallas_call | solution.py:685
  261.5 6.9 %down_own.1 = bf16[16,48,1536]{2,1,0:T(8,128)(2,1)} custom-call(s32[17]{0:T(128)} %pad_add_fusion.2.tab, bf16[768,1024]{1,0:T(8,128)(2,1)} %get-tuple-element.72.xt_ref, bf16[2,1024,1536]{2,1,0:T(8,128)(2,1)} %get-tuple-element.48.g_ref.y_ref), custom_call_target="tpu_custom_call" | custom-call | flops 2415919104 | bytes 7077888 | tf_op jit(solution)/shard_map/down_own/pallas_call | solution.py:541
  268.4 6.8 %up_own.1 = bf16[16,48,1536]{2,1,0:T(8,128)(2,1)} custom-call(s32[17]{0:T(128)} %pad_add_fusion.2.tab, bf16[768,1024]{1,0:T(8,128)(2,1)} %get-tuple-element.70.xt_ref, bf16[2,1024,1536]{2,1,0:T(8,128)(2,1)} %get-tuple-element.71.y_ref), custom_call_target="tpu_custom_call" | custom-call | flops 2415919104 | bytes 7077888 | tf_op jit(solution)/shard_map/up_own/pallas_call | solution.py:541
  275.2 8.8 %last_own.1 = bf16[16,48,1664]{2,1,0:T(8,128)(2,1)} custom-call(s32[17]{0:T(128)} %pad_add_fusion.2.tab, bf16[768,1024]{1,0:T(8,128)(2,1)} %get-tuple-element.64.tokt_ref, bf16[2,1024,1152]{2,1,0:T(8,128)(2,1)} %get-tuple-element.61.dqkv_ref, bf16[768,1024]{1,0:T(8,128)(2,1)} %get-tuple-element.65.dat_ref, bf16[2,1024,384]{2,1,0:T(8,128)(2,1)} %get-tuple-element.66.ctx_ref, ...), custom_call_target="tpu_custom_call" | custom-call | flops 2617245696 | bytes 12517376 | tf_op jit(solution)/shard_map/last_own/pallas_call | solution.py:650
  299.8 6.5 %collective-permute-done.36 = bf16[8,48,1536]{2,1,0:T(8,128)(2,1)S(1)} collective-permute-done((bf16[8,48,1536]{2,1,0:T(8,128)(2,1)S(1)}, bf16[8,48,1536]{2,1,0:T(8,128)(2,1)S(1)}, u32[]{:S(2)}, u32[]{:S(2)}) %collective-permute-start.36) | collective-permute-done | bytes 1179680 | tf_op jit(solution)/shard_map/ppermute | solution.py:98
  309.7 15.6 %collective-permute-done.31 = bf16[8,48,1536]{2,1,0:T(8,128)(2,1)S(1)} collective-permute-done((bf16[8,48,1536]{2,1,0:T(8,128)(2,1)S(1)}, bf16[8,48,1536]{2,1,0:T(8,128)(2,1)S(1)}, u32[]{:S(2)}, u32[]{:S(2)}) %collective-permute-start.31) | collective-permute-done | bytes 1179680 | tf_op jit(solution)/shard_map/ppermute | solution.py:98
  328.7 16.7 %collective-permute-done.26 = bf16[8,48,1664]{2,1,0:T(8,128)(2,1)S(1)} collective-permute-done((bf16[8,48,1664]{2,1,0:T(8,128)(2,1)S(1)}, bf16[8,48,1664]{2,1,0:T(8,128)(2,1)S(1)}, u32[]{:S(2)}, u32[]{:S(2)}) %collective-permute-start.26) | collective-permute-done | bytes 1277984 | tf_op jit(solution)/shard_map/ppermute | solution.py:98
  352.1 12.5 %collective-permute-done.38 = bf16[2,48,1536]{2,1,0:T(8,128)(2,1)S(1)} collective-permute-done((bf16[2,48,1536]{2,1,0:T(8,128)(2,1)S(1)}, bf16[2,48,1536]{2,1,0:T(8,128)(2,1)S(1)}, u32[]{:S(2)}, u32[]{:S(2)}) %collective-permute-start.38) | collective-permute-done | bytes 294944 | tf_op jit(solution)/shard_map/ppermute | solution.py:98
  369.9 8.9 %collective-permute-done.33 = bf16[2,48,1536]{2,1,0:T(8,128)(2,1)S(1)} collective-permute-done((bf16[2,48,1536]{2,1,0:T(8,128)(2,1)S(1)}, bf16[2,48,1536]{2,1,0:T(8,128)(2,1)S(1)}, u32[]{:S(2)}, u32[]{:S(2)}) %collective-permute-start.33) | collective-permute-done | bytes 294944 | tf_op jit(solution)/shard_map/ppermute | solution.py:98
  (223 shorter events, 145.6 us)
Async XLA Ops:
  14.5 16.4 %collective-permute-start.6 = (bf16[1,48,1536]{2,1,0:T(8,128)(2,1)S(1)}, bf16[1,48,1536]{2,1,0:T(8,128)(2,1)S(1)}, u32[]{:S(2)}, u32[]{:S(2)}) collective-permute-start(bf16[1,48,1536]{2,1,0:T(8,128)(2,1)S(1)} %convert_bitcast_fusion.1), channel_id=1, source_target_pairs={{0,8},{1,17},{2,10},{3,19},{4,12},{5,21},{6,14},{7,23},{8,0},{9,25... | collective-permute-start | bytes 442376 | tf_op jit(solution)/shard_map/ppermute | solution.py:84
  40.3 22.0 %collective-permute-start.3 = (bf16[8,48,1664]{2,1,0:T(8,128)(2,1)S(1)}, bf16[8,48,1664]{2,1,0:T(8,128)(2,1)S(1)}, u32[]{:S(2)}, u32[]{:S(2)}) collective-permute-start(bf16[8,48,1664]{2,1,0:T(8,128)(2,1)S(1)} %pad_maximum_fusion.2.w0), channel_id=1, source_target_pairs={{0,2},{1,5},{2,0},{3,7},{4,6},{5,1},{6,4},{7,3},{8,10},{9,13},{10,... | collective-permute-start | bytes 3833864 | tf_op jit(solution)/shard_map/ppermute | solution.py:84
  44.0 16.8 %collective-permute-start.8 = (bf16[4,48,1536]{2,1,0:T(8,128)(2,1)S(1)}, bf16[4,48,1536]{2,1,0:T(8,128)(2,1)S(1)}, u32[]{:S(2)}, u32[]{:S(2)}) collective-permute-start(bf16[4,48,1536]{2,1,0:T(8,128)(2,1)S(1)} %pad_maximum_fusion.6), channel_id=1, source_target_pairs={{0,4},{1,3},{2,6},{3,1},{4,0},{5,7},{6,2},{7,5},{8,12},{9,11},{10,... | collective-permute-start | bytes 1769480 | tf_op jit(solution)/shard_map/ppermute | solution.py:84
  48.8 24.7 %collective-permute-start.14 = (bf16[4,48,1536]{2,1,0:T(8,128)(2,1)S(1)}, bf16[4,48,1536]{2,1,0:T(8,128)(2,1)S(1)}, u32[]{:S(2)}, u32[]{:S(2)}) collective-permute-start(bf16[4,48,1536]{2,1,0:T(8,128)(2,1)S(1)} %pad_maximum_fusion.7), channel_id=1, source_target_pairs={{0,4},{1,3},{2,6},{3,1},{4,0},{5,7},{6,2},{7,5},{8,12},{9,11},{10,... | collective-permute-start | bytes 1769480 | tf_op jit(solution)/shard_map/ppermute | solution.py:84
  62.0 16.5 %collective-permute-start.9 = (bf16[8,48,1536]{2,1,0:T(8,128)(2,1)}, bf16[8,48,1536]{2,1,0:T(8,128)(2,1)}, u32[]{:S(2)}, u32[]{:S(2)}) collective-permute-start(bf16[8,48,1536]{2,1,0:T(8,128)(2,1)} %pad_maximum_fusion.3.w0.u0), channel_id=1, source_target_pairs={{0,2},{1,5},{2,0},{3,7},{4,6},{5,1},{6,4},{7,3},{8,10},{9,13},{10,... | collective-permute-start | bytes 3538952 | tf_op jit(solution)/shard_map/ppermute | solution.py:84
  62.1 29.1 %collective-permute-start.4 = (bf16[8,48,1664]{2,1,0:T(8,128)(2,1)S(1)}, bf16[8,48,1664]{2,1,0:T(8,128)(2,1)}, u32[]{:S(2)}, u32[]{:S(2)}) collective-permute-start(bf16[8,48,1664]{2,1,0:T(8,128)(2,1)S(1)} %pad_maximum_fusion.2.w0), channel_id=1, source_target_pairs={{0,1},{1,0},{2,3},{3,2},{4,5},{5,4},{6,7},{7,6},{8,9},{9,8},{10,11... | collective-permute-start | bytes 3833864 | tf_op jit(solution)/shard_map/ppermute | solution.py:76
  62.3 29.4 %collective-permute-start.5 = (bf16[8,48,1664]{2,1,0:T(8,128)(2,1)S(1)}, bf16[8,48,1664]{2,1,0:T(8,128)(2,1)}, u32[]{:S(2)}, u32[]{:S(2)}) collective-permute-start(bf16[8,48,1664]{2,1,0:T(8,128)(2,1)S(1)} %collective-permute-done.3.w1), channel_id=1, source_target_pairs={{0,1},{1,0},{2,3},{3,2},{4,5},{5,4},{6,7},{7,6},{8,9},{9,8},{10,11... | collective-permute-start | bytes 3833864 | tf_op jit(solution)/shard_map/ppermute | solution.py:76
  74.6 16.6 %collective-permute-start.15 = (bf16[8,48,1536]{2,1,0:T(8,128)(2,1)}, bf16[8,48,1536]{2,1,0:T(8,128)(2,1)}, u32[]{:S(2)}, u32[]{:S(2)}) collective-permute-start(bf16[8,48,1536]{2,1,0:T(8,128)(2,1)} %pad_maximum_fusion.4.w0.d0), channel_id=1, source_target_pairs={{0,2},{1,5},{2,0},{3,7},{4,6},{5,1},{6,4},{7,3},{8,10},{9,13},{10,... | collective-permute-start | bytes 3538952 | tf_op jit(solution)/shard_map/ppermute | solution.py:84
  75.2 34.7 %collective-permute-start.10 = (bf16[8,48,1536]{2,1,0:T(8,128)(2,1)}, bf16[8,48,1536]{2,1,0:T(8,128)(2,1)}, u32[]{:S(2)}, u32[]{:S(2)}) collective-permute-start(bf16[8,48,1536]{2,1,0:T(8,128)(2,1)} %pad_maximum_fusion.3.w0.u0), channel_id=1, source_target_pairs={{0,1},{1,0},{2,3},{3,2},{4,5},{5,4},{6,7},{7,6},{8,9},{9,8},{10,11... | collective-permute-start | bytes 3538952 | tf_op jit(solution)/shard_map/ppermute | solution.py:76
  78.6 31.4 %collective-permute-start.11 = (bf16[8,48,1536]{2,1,0:T(8,128)(2,1)}, bf16[8,48,1536]{2,1,0:T(8,128)(2,1)}, u32[]{:S(2)}, u32[]{:S(2)}) collective-permute-start(bf16[8,48,1536]{2,1,0:T(8,128)(2,1)} %collective-permute-done.9.w1.u1), channel_id=1, source_target_pairs={{0,1},{1,0},{2,3},{3,2},{4,5},{5,4},{6,7},{7,6},{8,9},{9,8},{10,11... | collective-permute-start | bytes 3538952 | tf_op jit(solution)/shard_map/ppermute | solution.py:76
  91.2 39.8 %collective-permute-start.16 = (bf16[8,48,1536]{2,1,0:T(8,128)(2,1)}, bf16[8,48,1536]{2,1,0:T(8,128)(2,1)S(1)}, u32[]{:S(2)}, u32[]{:S(2)}) collective-permute-start(bf16[8,48,1536]{2,1,0:T(8,128)(2,1)} %pad_maximum_fusion.4.w0.d0), channel_id=1, source_target_pairs={{0,1},{1,0},{2,3},{3,2},{4,5},{5,4},{6,7},{7,6},{8,9},{9,8},{10,11... | collective-permute-start | bytes 3538952 | tf_op jit(solution)/shard_map/ppermute | solution.py:76
  91.2 39.8 %collective-permute-start.17 = (bf16[8,48,1536]{2,1,0:T(8,128)(2,1)}, bf16[8,48,1536]{2,1,0:T(8,128)(2,1)S(1)}, u32[]{:S(2)}, u32[]{:S(2)}) collective-permute-start(bf16[8,48,1536]{2,1,0:T(8,128)(2,1)} %collective-permute-done.15.w1.d1), channel_id=1, source_target_pairs={{0,1},{1,0},{2,3},{3,2},{4,5},{5,4},{6,7},{7,6},{8,9},{9,8},{10,11... | collective-permute-start | bytes 3538952 | tf_op jit(solution)/shard_map/ppermute | solution.py:76
  166.9 117.2 %collective-permute-start.18 = (bf16[1024,768]{1,0:T(8,128)(2,1)}, bf16[1024,768]{1,0:T(8,128)(2,1)}, u32[]{:S(2)}, u32[]{:S(2)}) collective-permute-start(bf16[1024,768]{1,0:T(8,128)(2,1)} %bitcast.90), channel_id=1, source_target_pairs={{0,1},{1,0},{2,3},{3,2},{4,5},{5,4},{6,7},{7,6},{8,9},{9,8},{10,11... | collective-permute-start | bytes 4718600 | tf_op jit(solution)/shard_map/ppermute | solution.py:76
  189.6 98.0 %collective-permute-start.35 = (bf16[16,48,1536]{2,1,0:T(8,128)(2,1)}, bf16[16,48,1536]{2,1,0:T(8,128)(2,1)}, u32[]{:S(2)}, u32[]{:S(2)}) collective-permute-start(bf16[16,48,1536]{2,1,0:T(8,128)(2,1)} %down_other.1), channel_id=1, source_target_pairs={{0,1},{1,0},{2,3},{3,2},{4,5},{5,4},{6,7},{7,6},{8,9},{9,8},{10,11... | collective-permute-start | bytes 7077896 | tf_op jit(solution)/shard_map/ppermute | solution.py:76
  241.2 52.7 %collective-permute-start.25 = (bf16[16,48,1664]{2,1,0:T(8,128)(2,1)}, bf16[16,48,1664]{2,1,0:T(8,128)(2,1)}, u32[]{:S(2)}, u32[]{:S(2)}) collective-permute-start(bf16[16,48,1664]{2,1,0:T(8,128)(2,1)} %last_other.1), channel_id=1, source_target_pairs={{0,1},{1,0},{2,3},{3,2},{4,5},{5,4},{6,7},{7,6},{8,9},{9,8},{10,11... | collective-permute-start | bytes 7667720 | tf_op jit(solution)/shard_map/ppermute | solution.py:76
  248.5 42.0 %collective-permute-start.30 = (bf16[16,48,1536]{2,1,0:T(8,128)(2,1)}, bf16[16,48,1536]{2,1,0:T(8,128)(2,1)}, u32[]{:S(2)}, u32[]{:S(2)}) collective-permute-start(bf16[16,48,1536]{2,1,0:T(8,128)(2,1)} %up_other.1), channel_id=1, source_target_pairs={{0,1},{1,0},{2,3},{3,2},{4,5},{5,4},{6,7},{7,6},{8,9},{9,8},{10,11... | collective-permute-start | bytes 7077896 | tf_op jit(solution)/shard_map/ppermute | solution.py:76
  260.1 36.2 %collective-permute-start.24 = (f32[1024,768]{1,0:T(8,128)}, f32[1024,768]{1,0:T(8,128)S(1)}, u32[]{:S(2)}, u32[]{:S(2)}) collective-permute-start(f32[1024,768]{1,0:T(8,128)} %input_grads.1), channel_id=1, source_target_pairs={{0,1},{1,0},{2,3},{3,2},{4,5},{5,4},{6,7},{7,6},{8,9},{9,8},{10,11... | collective-permute-start | bytes 9437192 | tf_op jit(solution)/shard_map/ppermute | solution.py:76
  292.2 33.1 %collective-permute-start.31 = (bf16[8,48,1536]{2,1,0:T(8,128)(2,1)S(1)}, bf16[8,48,1536]{2,1,0:T(8,128)(2,1)S(1)}, u32[]{:S(2)}, u32[]{:S(2)}) collective-permute-start(bf16[8,48,1536]{2,1,0:T(8,128)(2,1)S(1)} %add_convert_fusion.7), channel_id=1, source_target_pairs={{0,2},{1,5},{2,0},{3,7},{4,6},{5,1},{6,4},{7,3},{8,10},{9,13},{10,... | collective-permute-start | bytes 3538952 | tf_op jit(solution)/shard_map/ppermute | solution.py:98
  295.4 49.9 %collective-permute-start.26 = (bf16[8,48,1664]{2,1,0:T(8,128)(2,1)S(1)}, bf16[8,48,1664]{2,1,0:T(8,128)(2,1)S(1)}, u32[]{:S(2)}, u32[]{:S(2)}) collective-permute-start(bf16[8,48,1664]{2,1,0:T(8,128)(2,1)S(1)} %add_convert_fusion.1), channel_id=1, source_target_pairs={{0,2},{1,5},{2,0},{3,7},{4,6},{5,1},{6,4},{7,3},{8,10},{9,13},{10,... | collective-permute-start | bytes 3833864 | tf_op jit(solution)/shard_map/ppermute | solution.py:98
  308.1 40.6 %collective-permute-start.37 = (bf16[4,48,1536]{2,1,0:T(8,128)(2,1)S(1)}, bf16[4,48,1536]{2,1,0:T(8,128)(2,1)S(1)}, u32[]{:S(2)}, u32[]{:S(2)}) collective-permute-start(bf16[4,48,1536]{2,1,0:T(8,128)(2,1)S(1)} %slice.199), channel_id=1, source_target_pairs={{0,4},{1,3},{2,6},{3,1},{4,0},{5,7},{6,2},{7,5},{8,12},{9,11},{10,... | collective-permute-start | bytes 1769480 | tf_op jit(solution)/shard_map/ppermute | solution.py:98
  327.1 22.6 %collective-permute-start.32 = (bf16[4,48,1536]{2,1,0:T(8,128)(2,1)S(1)}, bf16[4,48,1536]{2,1,0:T(8,128)(2,1)S(1)}, u32[]{:S(2)}, u32[]{:S(2)}) collective-permute-start(bf16[4,48,1536]{2,1,0:T(8,128)(2,1)S(1)} %slice.189), channel_id=1, source_target_pairs={{0,4},{1,3},{2,6},{3,1},{4,0},{5,7},{6,2},{7,5},{8,12},{9,11},{10,... | collective-permute-start | bytes 1769480 | tf_op jit(solution)/shard_map/ppermute | solution.py:98
  347.2 19.1 %collective-permute-start.27 = (bf16[4,48,1664]{2,1,0:T(8,128)(2,1)S(1)}, bf16[4,48,1664]{2,1,0:T(8,128)(2,1)S(1)}, u32[]{:S(2)}, u32[]{:S(2)}) collective-permute-start(bf16[4,48,1664]{2,1,0:T(8,128)(2,1)S(1)} %slice.177), channel_id=1, source_target_pairs={{0,4},{1,3},{2,6},{3,1},{4,0},{5,7},{6,2},{7,5},{8,12},{9,11},{10,... | collective-permute-start | bytes 1916936 | tf_op jit(solution)/shard_map/ppermute | solution.py:98
  349.9 28.9 %collective-permute-start.33 = (bf16[2,48,1536]{2,1,0:T(8,128)(2,1)S(1)}, bf16[2,48,1536]{2,1,0:T(8,128)(2,1)S(1)}, u32[]{:S(2)}, u32[]{:S(2)}) collective-permute-start(bf16[2,48,1536]{2,1,0:T(8,128)(2,1)S(1)} %slice.191), channel_id=1, source_target_pairs={{0,16},{1,9},{2,18},{3,11},{4,20},{5,13},{6,22},{7,15},{8,24},{9,1... | collective-permute-start | bytes 884744 | tf_op jit(solution)/shard_map/ppermute | solution.py:98
  364.8 18.1 %collective-permute-start.39 = (bf16[1,48,1536]{2,1,0:T(8,128)(2,1)S(1)}, bf16[1,48,1536]{2,1,0:T(8,128)(2,1)S(1)}, u32[]{:S(2)}, u32[]{:S(2)}) collective-permute-start(bf16[1,48,1536]{2,1,0:T(8,128)(2,1)S(1)} %slice.203), channel_id=1, source_target_pairs={{0,8},{1,17},{2,10},{3,19},{4,12},{5,21},{6,14},{7,23},{8,0},{9,25... | collective-permute-start | bytes 442376 | tf_op jit(solution)/shard_map/ppermute | solution.py:98
  (47 other events, 583.6 us)
